TPU v7x, 128 devices: a whole 4x4x4 slice. The times are simulated.
128 devices in a mesh: section: 2 (over y_lo), dp: 32 (over y_hi, z, x), mp: 2 (over core).
Axes of the slice: x: 4, y: 4 (y_hi: 2, y_lo: 2; y = y_hi * 2 + y_lo), z: 4, core: 2. Of those that a mesh axis runs over, the one named last changes fastest.
Arguments:
- inputs: bfloat16 [2, 32, 197, 768], P(None, 'dp'), may hold values from -6 to 6
- cotangent: bfloat16 [2, 32, 197, 768], P(None, 'dp'), may hold values from -6 to 6
- routes: int32 [2, 2, 32, 197, 2], P('section', None, 'dp'), may hold values from 0 to 3, all different within a row; in each aligned block of 197 rows (0 to 196, 197 to 393, ..., all dimensions but the last counted through in order) at most 128 rows name the same one
- gain_one: bfloat16 [2, 768], P('section', 'dp'), may hold values from 0.5 to 1.5
- shift_one: bfloat16 [2, 768], P('section', 'dp'), may hold values from -1 to 1
- qkv_weight: bfloat16 [2, 768, 3, 768], P('section', 'dp', None, 'mp'), may hold values from -0.3125 to 0.3125
- out_weight: bfloat16 [2, 768, 768], P('section', 'mp', 'dp'), may hold values from -0.75 to 0.75
- gain_two: bfloat16 [2, 768], P('section', 'dp'), may hold values from 0.5 to 1.5
- shift_two: bfloat16 [2, 768], P('section', 'dp'), may hold values from -1 to 1
- router: bfloat16 [2, 768, 4], P('section', 'dp'), may hold values from -0.15625 to 0.15625
- expert_in: bfloat16 [2, 4, 768, 3072], P('section', None, 'dp', 'mp'), may hold values from -0.21875 to 0.21875
- expert_out: bfloat16 [2, 4, 3072, 768], P('section', None, 'mp', 'dp'), may hold values from -0.4375 to 0.4375
Outputs:
- acts: bfloat16 [2, 2, 32, 197, 768], P('section', None, 'dp')
- input_grads: bfloat16 [2, 2, 32, 197, 768], P('section', None, 'dp')
- grad_gain_one: float32 [2, 768], P('section', 'dp')
- grad_shift_one: float32 [2, 768], P('section', 'dp')
- grad_qkv: float32 [2, 768, 3, 768], P('section', 'dp', None, 'mp')
- grad_out: float32 [2, 768, 768], P('section', 'mp', 'dp')
- grad_gain_two: float32 [2, 768], P('section', 'dp')
- grad_shift_two: float32 [2, 768], P('section', 'dp')
- grad_router: float32 [2, 768, 4], P('section', 'dp')
- grad_expert_in: float32 [2, 4, 768, 3072], P('section', None, 'dp', 'mp')
- grad_expert_out: float32 [2, 4, 3072, 768], P('section', None, 'mp', 'dp')
Inputs may be any that keep to these rules, and one draw needn't show every extreme that they name: Each token names 2 different experts. Among the 197 tokens of one micro-batch in one group of 1 consecutive images, no expert is named by more than 128 routes, and in some groups one expert is named by exactly 128.
All inputs are finite; a program needn't handle non-finite values.
Results may differ from a plain program's by a relative error of at most 0.035.
Values may be sent and summed in bfloat16 or wider, within the bound.
No kernel may reach another device: no remote copies, remote signals or barrier semaphores. Data moves between devices by JAX's collectives and lax.ppermute only.
A program may use at most 256 MiB of HBM per device.

v0:
```python
import jax
import jax.numpy as jnp
from jax import lax
from jax.sharding import PartitionSpec as P

HEAD_DIM = 64
SEQ = 197
CAP = 128


PRECISE = lax.Precision.HIGHEST
epsilon = 1e-06


def passed_along(block, axis, distance):
    devices = range(lax.axis_size(axis))
    route = [(i - distance, i) for i in devices if i - distance in devices]
    return lax.ppermute(block, axis, route)


def layer_norm(field, norm_gain, norm_shift):
    centered = field - jnp.mean(field, axis=-1, keepdims=True)
    spread = jnp.mean(centered * centered, axis=-1, keepdims=True)
    return centered * lax.rsqrt(spread + epsilon) * norm_gain + norm_shift


def route_slots(route_ids, capacity, experts):
    flattened = route_ids.reshape(-1)
    onehot = (flattened[:, None] == jnp.arange(experts, dtype=jnp.int32)[None, :]).astype(jnp.int32)
    before = jnp.cumsum(onehot, axis=0) - onehot
    position = jnp.sum(before * onehot, axis=1)
    return (flattened * capacity + position).reshape(route_ids.shape)


def forward_layer(weights, tokens, route_ids):
    (
        gain_one,
        shift_one,
        qkv_matrix,
        out_matrix,
        gain_two,
        shift_two,
        router_matrix,
        expert_first,
        expert_second,
    ) = weights
    token_count = tokens.shape[0]
    experts = expert_first.shape[0]
    images = token_count // SEQ
    local_heads = qkv_matrix.shape[2] // HEAD_DIM
    slot_ids = route_slots(route_ids, CAP, experts)
    normed_one = layer_norm(
        tokens, gain_one.astype(jnp.float32), shift_one.astype(jnp.float32)
    ).astype(jnp.bfloat16)
    projected = jnp.einsum(
        "td,dcf->tcf", normed_one, qkv_matrix, preferred_element_type=jnp.float32
    ).astype(jnp.bfloat16)
    split_heads = projected.reshape(images, SEQ, 3, local_heads, HEAD_DIM)
    queries = split_heads[:, :, 0]
    keys_all = split_heads[:, :, 1]
    values_all = split_heads[:, :, 2]
    scores = jnp.einsum(
        "bqhe,bkhe->bhqk", queries, keys_all, preferred_element_type=jnp.float32
    ) * HEAD_DIM ** (-0.5)
    probability = jax.nn.softmax(scores, axis=-1)
    prob_low = probability.astype(jnp.bfloat16)
    mixed_heads = jnp.einsum(
        "bhqk,bkhe->bqhe", prob_low, values_all, preferred_element_type=jnp.float32
    ).astype(jnp.bfloat16)
    mixed_heads = mixed_heads.reshape(token_count, local_heads * HEAD_DIM)
    attended = lax.psum(jnp.dot(mixed_heads, out_matrix, preferred_element_type=jnp.float32), "mp")
    hidden = tokens + attended
    normed_two = layer_norm(
        hidden, gain_two.astype(jnp.float32), shift_two.astype(jnp.float32)
    ).astype(jnp.bfloat16)
    gate_probs = jax.nn.softmax(
        jnp.dot(normed_two, router_matrix, preferred_element_type=jnp.float32), axis=-1
    )
    chosen = jnp.take_along_axis(gate_probs, route_ids, axis=1)
    slot_range = jnp.arange(experts * CAP, dtype=jnp.int32)
    placing = jnp.sum(
        (slot_ids[None, :, :] == slot_range[:, None, None]).astype(jnp.bfloat16), axis=2
    )
    dispatched = (
        jnp.dot(placing, normed_two, preferred_element_type=jnp.float32)
        .astype(jnp.bfloat16)
        .reshape(experts, CAP, -1)
    )
    inner_pre = jnp.einsum(
        "ecd,edf->ecf", dispatched, expert_first, preferred_element_type=jnp.float32
    )
    activated = jax.nn.gelu(inner_pre, approximate=False).astype(jnp.bfloat16)
    partial_out = jnp.einsum(
        "ecf,efd->ecd", activated, expert_second, preferred_element_type=jnp.float32
    )
    expert_sum = lax.psum(partial_out, "mp").reshape(experts * CAP, -1)
    picked = jnp.take(expert_sum, slot_ids, axis=0)
    output = hidden + jnp.sum(chosen[:, :, None] * picked, axis=1)
    saved = (
        tokens,
        normed_one,
        queries,
        keys_all,
        values_all,
        probability,
        prob_low,
        mixed_heads,
        hidden,
        normed_two,
        gate_probs,
        chosen,
        picked,
        slot_ids,
        dispatched,
        inner_pre,
        activated,
    )
    return (output, saved)


def backward_experts(weights, saved, grad_output):
    expert_first, expert_second = (weights[7], weights[8])
    (
        tokens,
        normed_one,
        queries,
        keys_all,
        values_all,
        probability,
        prob_low,
        mixed_heads,
        hidden,
        normed_two,
        gate_probs,
        chosen,
        picked,
        slot_ids,
        dispatched,
        inner_pre,
        activated,
    ) = saved
    experts = expert_first.shape[0]
    width = tokens.shape[1]
    grad_chosen = jnp.sum(grad_output[:, None, :] * picked, axis=2)
    grad_picked = (
        (chosen[:, :, None] * grad_output[:, None, :]).astype(jnp.bfloat16).reshape(-1, width)
    )
    slot_range = jnp.arange(experts * CAP, dtype=jnp.int32)
    selector = (slot_ids.reshape(-1)[None, :] == slot_range[:, None]).astype(jnp.bfloat16)
    grad_expert = (
        jnp.dot(selector, grad_picked, preferred_element_type=jnp.float32)
        .astype(jnp.bfloat16)
        .reshape(experts, CAP, width)
    )
    grad_act = jnp.einsum(
        "ecd,efd->ecf", grad_expert, expert_second, preferred_element_type=jnp.float32
    )
    grad_second = jnp.einsum(
        "ecf,ecd->efd", activated, grad_expert, preferred_element_type=jnp.float32
    )
    unused, gelu_back = jax.vjp(lambda field: jax.nn.gelu(field, approximate=False), inner_pre)
    grad_inner = gelu_back(grad_act)[0].astype(jnp.bfloat16)
    grad_first = jnp.einsum(
        "ecd,ecf->edf", dispatched, grad_inner, preferred_element_type=jnp.float32
    )
    grad_dispatched = jnp.einsum(
        "ecf,edf->ecd", grad_inner, expert_first, preferred_element_type=jnp.float32
    ).reshape(experts * CAP, width)
    grad_returned = jnp.sum(jnp.take(grad_dispatched, slot_ids, axis=0), axis=1)
    grad_norm_two = lax.psum(grad_returned, "mp")
    return (grad_norm_two, grad_chosen, (grad_first, grad_second))


def backward_dense(weights, saved, grad_output, grad_norm_two, grad_chosen):
    (
        gain_one,
        shift_one,
        qkv_matrix,
        out_matrix,
        gain_two,
        shift_two,
        router_matrix,
        expert_first,
        expert_second,
    ) = weights
    (
        tokens,
        normed_one,
        queries,
        keys_all,
        values_all,
        probability,
        prob_low,
        mixed_heads,
        hidden,
        normed_two,
        gate_probs,
        chosen,
        picked,
        slot_ids,
        dispatched,
        inner_pre,
        activated,
    ) = saved
    token_count = tokens.shape[0]
    experts = expert_first.shape[0]
    expert_ids = slot_ids // CAP
    expert_range = jnp.arange(experts, dtype=jnp.int32)
    grad_gates = jnp.sum(
        (expert_ids[:, :, None] == expert_range[None, None, :]).astype(jnp.float32)
        * grad_chosen[:, :, None],
        axis=1,
    )
    grad_logits = gate_probs * (
        grad_gates - jnp.sum(gate_probs * grad_gates, axis=-1, keepdims=True)
    )
    grad_router = jnp.dot(normed_two.astype(jnp.float32).T, grad_logits, precision=PRECISE)
    grad_norm_two = grad_norm_two + jnp.dot(
        grad_logits, router_matrix.astype(jnp.float32).T, precision=PRECISE
    )
    unused_two, norm_back_two = jax.vjp(
        layer_norm, hidden, gain_two.astype(jnp.float32), shift_two.astype(jnp.float32)
    )
    grad_hidden_part, grad_gain_two, grad_shift_two = norm_back_two(grad_norm_two)
    grad_hidden = grad_output + grad_hidden_part
    grad_attended = grad_hidden.astype(jnp.bfloat16)
    grad_out_matrix = jnp.einsum(
        "tf,td->fd", mixed_heads, grad_attended, preferred_element_type=jnp.float32
    )
    grad_mixed = jnp.einsum(
        "td,fd->tf", grad_attended, out_matrix, preferred_element_type=jnp.float32
    ).astype(jnp.bfloat16)
    grad_mixed = grad_mixed.reshape(queries.shape)
    grad_prob = jnp.einsum(
        "bqhe,bkhe->bhqk", grad_mixed, values_all, preferred_element_type=jnp.float32
    )
    grad_values = jnp.einsum(
        "bhqk,bqhe->bkhe", prob_low, grad_mixed, preferred_element_type=jnp.float32
    )
    grad_scores = (
        probability * (grad_prob - jnp.sum(probability * grad_prob, axis=-1, keepdims=True))
    ).astype(jnp.bfloat16)
    grad_queries = jnp.einsum(
        "bhqk,bkhe->bqhe", grad_scores, keys_all, preferred_element_type=jnp.float32
    ) * HEAD_DIM ** (-0.5)
    grad_keys = jnp.einsum(
        "bhqk,bqhe->bkhe", grad_scores, queries, preferred_element_type=jnp.float32
    ) * HEAD_DIM ** (-0.5)
    grad_projected = (
        jnp.stack([grad_queries, grad_keys, grad_values], axis=2)
        .astype(jnp.bfloat16)
        .reshape(token_count, 3, -1)
    )
    grad_qkv_matrix = jnp.einsum(
        "td,tcf->dcf", normed_one, grad_projected, preferred_element_type=jnp.float32
    )
    grad_norm_one = lax.psum(
        jnp.einsum("tcf,dcf->td", grad_projected, qkv_matrix, preferred_element_type=jnp.float32),
        "mp",
    )
    unused_one, norm_back_one = jax.vjp(
        layer_norm, tokens, gain_one.astype(jnp.float32), shift_one.astype(jnp.float32)
    )
    grad_tokens_part, grad_gain_one, grad_shift_one = norm_back_one(grad_norm_one)
    grads = (
        grad_gain_one,
        grad_shift_one,
        grad_qkv_matrix,
        grad_out_matrix,
        grad_gain_two,
        grad_shift_two,
        grad_router,
    )
    return (grad_hidden + grad_tokens_part, grads)


def shards(
    inputs,
    cotangent,
    routes,
    gain_one,
    shift_one,
    qkv_weight,
    out_weight,
    gain_two,
    shift_two,
    router,
    expert_in,
    expert_out,
):
    section_index = lax.axis_index("section")
    last_section = lax.axis_size("section") - 1
    micro_count = inputs.shape[0]
    token_count = inputs.shape[1] * inputs.shape[2]
    width = inputs.shape[3]
    dense_full = (
        lax.all_gather(gain_one[0], "dp", axis=0, tiled=True),
        lax.all_gather(shift_one[0], "dp", axis=0, tiled=True),
        lax.all_gather(qkv_weight[0], "dp", axis=0, tiled=True),
        lax.all_gather(out_weight[0], "dp", axis=1, tiled=True),
        lax.all_gather(gain_two[0], "dp", axis=0, tiled=True),
        lax.all_gather(shift_two[0], "dp", axis=0, tiled=True),
        lax.all_gather(router[0], "dp", axis=0, tiled=True),
    )
    expert_full = (
        lax.all_gather(expert_in[0], "dp", axis=1, tiled=True),
        lax.all_gather(expert_out[0], "dp", axis=2, tiled=True),
    )
    weights = tuple(dense_full) + tuple(expert_full)
    own_inputs = inputs.reshape(micro_count, token_count, width)
    own_grads = cotangent.reshape(micro_count, token_count, width)
    all_paths = routes[0].reshape(micro_count, token_count, routes.shape[-1])
    received = jnp.zeros((token_count, width), jnp.bfloat16)
    outputs_list = []
    saved_list = []
    for moment in range(micro_count + 1):
        micro_here = jnp.clip(moment - section_index, 0, micro_count - 1)
        layer_input = jnp.where(
            section_index == 0, own_inputs[min(moment, micro_count - 1)], received
        )
        paths_here = lax.dynamic_index_in_dim(all_paths, micro_here, 0, keepdims=False)
        output, saved = forward_layer(weights, layer_input.astype(jnp.float32), paths_here)
        output_low = output.astype(jnp.bfloat16)
        outputs_list.append(output_low)
        saved_list.append(saved)
        if moment < micro_count:
            received = passed_along(output_low, "section", 1)
    saved_stack = jax.tree.map(lambda *pieces: jnp.stack(pieces), *saved_list)
    acts_local = lax.dynamic_slice_in_dim(
        jnp.stack(outputs_list), section_index, micro_count, 0
    ).reshape(inputs.shape)[None]
    dense_back = (
        lax.all_gather(gain_one[0], "dp", axis=0, tiled=True),
        lax.all_gather(shift_one[0], "dp", axis=0, tiled=True),
        lax.all_gather(qkv_weight[0], "dp", axis=0, tiled=True),
        lax.all_gather(out_weight[0], "dp", axis=1, tiled=True),
        lax.all_gather(gain_two[0], "dp", axis=0, tiled=True),
        lax.all_gather(shift_two[0], "dp", axis=0, tiled=True),
        lax.all_gather(router[0], "dp", axis=0, tiled=True),
    )
    expert_again = (
        lax.all_gather(expert_in[0], "dp", axis=1, tiled=True),
        lax.all_gather(expert_out[0], "dp", axis=2, tiled=True),
    )
    back_weights = tuple(dense_back) + tuple(expert_again)
    grad_received = jnp.zeros((token_count, width), jnp.bfloat16)
    grad_list = []
    dense_totals = None
    expert_totals = None
    for moment in range(micro_count + 1):
        micro_here = moment - 1 + section_index
        valid_flag = ((micro_here >= 0) & (micro_here < micro_count)).astype(jnp.float32)
        index_here = jnp.clip(micro_here, 0, micro_count - 1)
        incoming = (
            jnp.where(
                section_index == last_section,
                own_grads[min(moment, micro_count - 1)],
                grad_received,
            ).astype(jnp.float32)
            * valid_flag
        )
        saved = jax.tree.map(
            lambda member: lax.dynamic_index_in_dim(
                member, index_here + section_index, 0, keepdims=False
            ),
            saved_stack,
        )
        grad_norm_two, grad_chosen, expert_grads = backward_experts(back_weights, saved, incoming)
        if expert_totals is None:
            expert_totals = expert_grads
        else:
            expert_totals = jax.tree.map(jnp.add, expert_totals, expert_grads)
        grad_input, dense_grads = backward_dense(
            back_weights, saved, incoming, grad_norm_two, grad_chosen
        )
        if dense_totals is None:
            dense_totals = dense_grads
        else:
            dense_totals = jax.tree.map(jnp.add, dense_totals, dense_grads)
        grad_low = grad_input.astype(jnp.bfloat16)
        grad_list.append(grad_low)
        if moment < micro_count:
            grad_received = passed_along(grad_low, "section", -1)
    input_local = lax.dynamic_slice_in_dim(
        jnp.stack(grad_list), 1 - section_index, micro_count, 0
    ).reshape(inputs.shape)[None]
    summed = (
        lax.psum_scatter(dense_totals[0], "dp", scatter_dimension=0, tiled=True),
        lax.psum_scatter(dense_totals[1], "dp", scatter_dimension=0, tiled=True),
        lax.psum_scatter(dense_totals[2], "dp", scatter_dimension=0, tiled=True),
        lax.psum_scatter(dense_totals[3], "dp", scatter_dimension=1, tiled=True),
        lax.psum_scatter(dense_totals[4], "dp", scatter_dimension=0, tiled=True),
        lax.psum_scatter(dense_totals[5], "dp", scatter_dimension=0, tiled=True),
        lax.psum_scatter(dense_totals[6], "dp", scatter_dimension=0, tiled=True),
        lax.psum_scatter(expert_totals[0], "dp", scatter_dimension=1, tiled=True),
        lax.psum_scatter(expert_totals[1], "dp", scatter_dimension=2, tiled=True),
    )
    return (acts_local, input_local) + tuple((member[None] for member in summed))


def solution(mesh):
    placed = (
        P(None, "dp", None, None),
        P(None, "dp", None, None),
        P("section", None, "dp", None, None),
        P("section", "dp"),
        P("section", "dp"),
        P("section", "dp", None, "mp"),
        P("section", "mp", "dp"),
        P("section", "dp"),
        P("section", "dp"),
        P("section", "dp", None),
        P("section", None, "dp", "mp"),
        P("section", None, "mp", "dp"),
    )
    return jax.shard_map(
        shards,
        mesh=mesh,
        in_specs=placed,
        out_specs=(
            P("section", None, "dp", None, None),
            P("section", None, "dp", None, None),
            P("section", "dp"),
            P("section", "dp"),
            P("section", "dp", None, "mp"),
            P("section", "mp", "dp"),
            P("section", "dp"),
            P("section", "dp"),
            P("section", "dp", None),
            P("section", None, "dp", "mp"),
            P("section", None, "mp", "dp"),
        ),
        check_vma=False,
    )
```

profile of v0, /device:TPU:16, one launch (start us, length us, event | category | flops | bytes accessed | tf_op | source)
XLA Modules:
  0.0 2087.2 jit_solution(11000441533195501870)
XLA Ops:
  13.3 96.2 %all-reduce.15 = (bf16[768]{0:T(1024)(128)(2,1)S(1)}, bf16[768]{0:T(1024)(128)(2,1)S(1)}, bf16[768]{0:T(1024)(128)(2,1)S(1)}, bf16[768]{0:T(1024)(128)(2,1)S(1)}) all-reduce(bf16[768]{0:T(1024)(128)(2,1)S(1)} %dynamic-update-slice.3, bf16[768]{0:T(1024)(128)(2,1)S(1)} %dynamic-update-slice.2, ...), channel_id=7, replica_groups=mesh['section'=2,'dp'=32,'mp'=2] {'dp'}, use_global_device_ids=true, to_apply=%add.6 | all-reduce | flops 3072 | bytes 12288
  113.3 90.5 %all-gather.3 = bf16[1,384,768]{1,2,0:T(8,128)(2,1)S(1)} all-gather(bf16[1,384,24]{1,2,0:T(8,128)(2,1)S(1)} %copy-done.147), channel_id=5, replica_groups=mesh['section'=2,'dp'=32,'mp'=2] {'dp'}, dimensions={2}, use_global_device_ids=true | all-gather | bytes 608256 | tf_op jit(solution)/shard_map/all_gather | solution.py:300
  222.0 92.6 %all-gather.6 = bf16[1,768,4]{2,0,1:T(2,128)(2,1)S(1)} all-gather(bf16[1,24,4]{2,0,1:T(2,128)(2,1)S(1)} %copy.523), channel_id=8, replica_groups=mesh['section'=2,'dp'=32,'mp'=2] {'dp'}, dimensions={1}, use_global_device_ids=true | all-gather | bytes 6336 | tf_op jit(solution)/shard_map/all_gather | solution.py:303
  321.6 26.8 %all-gather.17.cloned.1.call-done = bf16[1,4,1536,768]{2,1,0,3:T(4,128)(2,1)} async-done(((bf16[1,4,1536,24]{2,1,0,3:T(4,128)(2,1)}), bf16[1,4,1536,768]{2,1,0,3:T(4,128)(2,1)}) %all-gather.17.cloned.1.call-update) | async-done | bytes 9437200 | tf_op jit(solution)/shard_map/all_gather | solution.py:307
  348.4 15.5 copy.532
  363.9 95.2 %all-gather.15.cloned.1.call-done = bf16[1,4,768,1536]{3,2,1,0:T(8,128)(2,1)} async-done(((bf16[1,4,24,1536]{3,2,1,0:T(8,128)(2,1)}), bf16[1,4,768,1536]{3,2,1,0:T(8,128)(2,1)}) %all-gather.15.cloned.1.call-update) | async-done | bytes 9437200 | tf_op jit(solution)/shard_map/all_gather | solution.py:306
  465.5 9.4 fusion.13
  482.1 19.2 all-reduce.30.cloned.1.call-done
  538.2 24.8 %all-reduce.32.cloned.1.call-done = f32[197,768]{1,0:T(8,128)} async-done(((f32[197,768]{1,0:T(8,128)}), f32[197,768]{1,0:T(8,128)}) %all-reduce.32.cloned.1.call-update) | async-done | bytes 605200 | tf_op jit(solution)/shard_map/psum | solution.py:71
  574.6 9.4 fusion.11
  598.3 13.2 all-reduce.34.cloned.1.call-done
  648.6 23.5 %all-reduce.36.cloned.1.call-done = f32[197,768]{1,0:T(8,128)} async-done(((f32[197,768]{1,0:T(8,128)}), f32[197,768]{1,0:T(8,128)}) %all-reduce.36.cloned.1.call-update) | async-done | bytes 605200 | tf_op jit(solution)/shard_map/psum | solution.py:71
  696.5 11.9 fusion.40
  716.3 12.0 fusion.9
  744.1 15.2 all-reduce.48.cloned.1.call-done
  792.7 25.6 %all-reduce.38.cloned.1.call-done = f32[197,768]{1,0:T(8,128)} async-done(((f32[197,768]{1,0:T(8,128)}), f32[197,768]{1,0:T(8,128)}) %all-reduce.38.cloned.1.call-update) | async-done | bytes 605200 | tf_op jit(solution)/shard_map/psum | solution.py:257
  826.2 9.7 collective-permute-done.2
  844.9 11.9 fusion.45
  871.7 23.7 %all-reduce.40.cloned.1.call-done = f32[197,768]{1,0:T(8,128)} async-done(((f32[197,768]{1,0:T(8,128)}), f32[197,768]{1,0:T(8,128)}) %all-reduce.40.cloned.1.call-update) | async-done | bytes 605200 | tf_op jit(solution)/shard_map/psum | solution.py:170
  914.1 25.8 %all-reduce.42.cloned.1.call-done = f32[197,768]{1,0:T(8,128)} async-done(((f32[197,768]{1,0:T(8,128)}), f32[197,768]{1,0:T(8,128)}) %all-reduce.42.cloned.1.call-update) | async-done | bytes 605200 | tf_op jit(solution)/shard_map/psum | solution.py:257
  962.3 11.9 fusion.50
  989.3 23.5 %all-reduce.44.cloned.1.call-done = f32[197,768]{1,0:T(8,128)} async-done(((f32[197,768]{1,0:T(8,128)}), f32[197,768]{1,0:T(8,128)}) %all-reduce.44.cloned.1.call-update) | async-done | bytes 605200 | tf_op jit(solution)/shard_map/psum | solution.py:170
  1040.5 7.9 fusion.197
  1048.5 8.2 fusion.195
  1056.7 20.5 add_add_fusion.1
  1101.6 7.9 fusion.147
  1109.5 8.0 fusion.145
  1117.5 20.9 %add_add_fusion = f32[4,1536,768]{1,2,0:T(8,128)} fusion(f32[4,1536,768]{1,2,0:T(8,128)} %fusion.147, f32[4,1536,768]{1,2,0:T(8,128)} %fusion.145, bf16[4,128,768]{2,1,0:T(8,128)(2,1)S(1)} %bitcast.1098, bf16[3,4,128,1536]{3,2,1,0:T(8,128)(2,1)} %copy-done.9, s32[]{:T(128)S(6)} %select_n.182), kind=kOutput, calls=%fused_computation.12 | convolution fusion | flops 1217396736 | bytes 58982404 | tf_op jit(solution)/shard_map/ecf,ecd->efd/dot_general | solution.py:158
  1148.0 181.5 %all-reduce.13 = (f32[768]{0:T(1024)S(1)}, f32[768]{0:T(1024)S(1)}, f32[768]{0:T(1024)S(1)}, f32[768]{0:T(1024)S(1)}, f32[768,4]{0,1:T(4,128)S(1)}) all-reduce(f32[768]{0:T(1024)S(1)} %add_add_fusion.15, f32[768]{0:T(1024)S(1)} %add_add_fusion.14, ...), channel_id=11, replica_groups=mesh['section'=2,'dp'=32,'mp'=2] {'dp'}, use_global_device_ids=true, to_apply=%region_93.96.clone | all-reduce | flops 6144 | bytes 49152
  1332.5 181.5 %reduce-scatter.8.cloned.1.call-done = f32[24,3,384]{2,0,1:T(8,128)} async-done(((f32[768,3,384]{2,0,1:T(8,128)}), f32[24,3,384]{2,0,1:T(8,128)}) %reduce-scatter.8.cloned.1.call-update) | async-done | bytes 110608 | tf_op jit(solution)/shard_map/reduce_scatter | solution.py:390
  1514.0 283.4 %reduce-scatter.10.cloned.1.call-done = f32[4,24,1536]{2,1,0:T(8,128)} async-done(((f32[4,768,1536]{2,1,0:T(8,128)}), f32[4,24,1536]{2,1,0:T(8,128)}) %reduce-scatter.10.cloned.1.call-update) | async-done | bytes 589840 | tf_op jit(solution)/shard_map/reduce_scatter | solution.py:395
  1797.4 282.8 %reduce-scatter.12.cloned.1.call-done = f32[4,1536,24]{1,2,0:T(8,128)} async-done(((f32[4,1536,768]{1,2,0:T(8,128)}), f32[4,1536,24]{1,2,0:T(8,128)}) %reduce-scatter.12.cloned.1.call-update) | async-done | bytes 589840 | tf_op jit(solution)/shard_map/reduce_scatter | solution.py:396
  (846 shorter events, 377.4 us)
Async XLA Ops:
  7.2 106.1 %copy-start.147 = (bf16[1,384,24]{1,2,0:T(8,128)(2,1)S(1)}, bf16[1,384,24]{1,2,0:T(8,128)(2,1)}, u32[]{:S(2)}) copy-start(bf16[1,384,24]{1,2,0:T(8,128)(2,1)} %param.22) | copy-start | bytes 55300
  7.2 196.7 %all-gather.13.cloned.1.call-start = ((), (), s32[]{:S(2)}) async-start(), calls=%async_computation.17 | async-start | bytes 1824768 | tf_op jit(solution)/shard_map/all_gather | solution.py:299
  7.9 308.8 %all-reduce.28.cloned.1.call-start = ((), (), s32[]{:S(2)}) async-start(), calls=%async_computation.4 | async-start | bytes 1228800 | tf_op jit(solution)/shard_map/psum | solution.py:71
  111.9 414.6 %copy-start.51 = (bf16[1,1,197,768]{3,0,2,1:T(2,128)(2,1)}, bf16[1,1,197,768]{3,0,2,1:T(2,128)(2,1)S(1)}, u32[]{:S(2)}) copy-start(bf16[1,1,197,768]{3,0,2,1:T(2,128)(2,1)S(1)} %get-tuple-element.180) | copy-start | bytes 907780
  112.9 403.4 %copy-start.7 = (bf16[1,1,197,768]{3,2,1,0:T(8,128)(2,1)}, bf16[1,1,197,768]{3,2,1,0:T(8,128)(2,1)S(1)}, u32[]{:S(2)}) copy-start(bf16[1,1,197,768]{3,2,1,0:T(8,128)(2,1)S(1)} %get-tuple-element.139) | copy-start | bytes 907780
  113.1 94.8 %copy-start.174 = (f32[197]{0:T(256)}, f32[197]{0:T(256)S(1)}, u32[]{:S(2)}) copy-start(f32[197]{0:T(256)S(1)} %broadcast_multiply_fusion.11) | copy-start | bytes 2368
  113.3 92.9 %copy-start.185 = (f32[197]{0:T(256)}, f32[197]{0:T(256)S(1)}, u32[]{:S(2)}) copy-start(f32[197]{0:T(256)S(1)} %add_rsqrt_fusion.5) | copy-start | bytes 2368
  212.0 136.4 %all-gather.17.cloned.1.call-start = ((), (), s32[]{:S(2)}) async-start(), calls=%async_computation.19 | async-start | bytes 9732096 | tf_op jit(solution)/shard_map/all_gather | solution.py:307
  213.0 246.1 %all-gather.15.cloned.1.call-start = ((), (), s32[]{:S(2)}) async-start(), calls=%async_computation.18 | async-start | bytes 9732096 | tf_op jit(solution)/shard_map/all_gather | solution.py:306
  213.5 287.8 %all-reduce.30.cloned.1.call-start = ((), (), s32[]{:S(2)}) async-start(), calls=%async_computation.5 | async-start | bytes 3145728 | tf_op jit(solution)/shard_map/psum | solution.py:96
  321.2 154.3 %copy-start.56 = (bf16[197,768]{1,0:T(8,128)(2,1)}, bf16[197,768]{1,0:T(8,128)(2,1)S(1)}, u32[]{:S(2)}) copy-start(bf16[197,768]{1,0:T(8,128)(2,1)S(1)} %add_convert_fusion.9) | copy-start | bytes 907780
  321.6 137.5 %copy-start.69 = (bf16[512,768]{1,0:T(8,128)(2,1)}, bf16[512,768]{1,0:T(8,128)(2,1)S(1)}, u32[]{:S(2)}) copy-start(bf16[512,768]{1,0:T(8,128)(2,1)S(1)} %convolution_convert_fusion.2) | copy-start | bytes 2359300
  474.9 88.1 %all-reduce.32.cloned.1.call-start = ((), (), s32[]{:S(2)}) async-start(), calls=%async_computation.6 | async-start | bytes 1228800 | tf_op jit(solution)/shard_map/psum | solution.py:71
  516.5 10.1 collective-permute-start
  536.0 75.6 %all-reduce.34.cloned.1.call-start = ((), (), s32[]{:S(2)}) async-start(), calls=%async_computation.7 | async-start | bytes 3145728 | tf_op jit(solution)/shard_map/psum | solution.py:96
  584.0 88.2 %all-reduce.36.cloned.1.call-start = ((), (), s32[]{:S(2)}) async-start(), calls=%async_computation.8 | async-start | bytes 1228800 | tf_op jit(solution)/shard_map/psum | solution.py:71
  625.9 10.1 collective-permute-start.1
  645.2 114.1 %all-reduce.48.cloned.1.call-start = ((), (), s32[]{:S(2)}) async-start(), calls=%async_computation.21 | async-start | bytes 4374528 | tf_op jit(solution)/shard_map/psum | solution.py:96
  730.8 87.5 %all-reduce.38.cloned.1.call-start = ((), (), s32[]{:S(2)}) async-start(), calls=%async_computation.9 | async-start | bytes 1228800 | tf_op jit(solution)/shard_map/psum | solution.py:257
  743.0 35.5 %copy-start = (f32[3,197,768]{2,1,0:T(8,128)}, f32[3,197,768]{2,1,0:T(8,128)S(1)}, u32[]{:S(2)}) copy-start(f32[3,197,768]{2,1,0:T(8,128)S(1)} %pad_maximum_fusion.5) | copy-start | bytes 5446660
  778.9 44.2 %copy-start.168 = (f32[197]{0:T(256)}, f32[197]{0:T(256)S(1)}, u32[]{:S(2)}) copy-start(f32[197]{0:T(256)S(1)} %negate_multiply_fusion.11) | copy-start | bytes 2368
  792.3 103.1 %all-reduce.40.cloned.1.call-start = ((), (), s32[]{:S(2)}) async-start(), calls=%async_computation.10 | async-start | bytes 1228800 | tf_op jit(solution)/shard_map/psum | solution.py:170
  824.6 11.4 collective-permute-start.2
  826.2 69.2 %copy-start.148 = (f32[197]{0:T(256)}, f32[197]{0:T(256)S(1)}, u32[]{:S(2)}) copy-start(f32[197]{0:T(256)S(1)} %broadcast_multiply_fusion.1) | copy-start | bytes 2368
  869.5 70.4 %all-reduce.42.cloned.1.call-start = ((), (), s32[]{:S(2)}) async-start(), calls=%async_computation.11 | async-start | bytes 1228800 | tf_op jit(solution)/shard_map/psum | solution.py:257
  913.9 98.9 %all-reduce.44.cloned.1.call-start = ((), (), s32[]{:S(2)}) async-start(), calls=%async_computation.12 | async-start | bytes 1228800 | tf_op jit(solution)/shard_map/psum | solution.py:170
  943.5 11.4 collective-permute-start.3
  986.8 156.5 %all-reduce.46.cloned.1.call-start = ((), (), s32[]{:S(2)}) async-start(), calls=%async_computation.13 | async-start | bytes 1228800 | tf_op jit(solution)/shard_map/psum | solution.py:257
  1030.1 302.4 %reduce-scatter.14.cloned.1.call-start = ((), (), s32[]{:S(2)}) async-start(), calls=%async_computation.20 | async-start | bytes 1216512
  1032.7 481.3 %reduce-scatter.8.cloned.1.call-start = ((), (), s32[]{:S(2)}) async-start(), calls=%async_computation.14 | async-start | bytes 3649536 | tf_op jit(solution)/shard_map/reduce_scatter | solution.py:390
  1037.8 759.7 %reduce-scatter.10.cloned.1.call-start = ((), (), s32[]{:S(2)}) async-start(), calls=%async_computation.15 | async-start | bytes 19464192 | tf_op jit(solution)/shard_map/reduce_scatter | solution.py:395
  1077.2 1003.0 %reduce-scatter.12.cloned.1.call-start = ((), (), s32[]{:S(2)}) async-start(), calls=%async_computation.16 | async-start | bytes 19464192 | tf_op jit(solution)/shard_map/reduce_scatter | solution.py:396
  (198 other events, 1817.1 us)
Sparse Core Ops, SparseCore 0:
  11.0 69.7 all-gather.12
  212.1 23.0 all-reduce.27
  238.9 109.4 all-gather.16
  351.3 107.7 all-gather.14
  475.0 26.2 all-reduce.29
  536.1 26.8 all-reduce.31
  584.1 27.3 all-reduce.33
  645.3 26.8 all-reduce.35
  730.9 28.3 all-reduce.47
  792.5 25.7 all-reduce.37
  869.6 25.7 all-reduce.39
  914.0 25.7 all-reduce.41
  986.9 25.7 all-reduce.43
  1030.3 25.7 all-reduce.45
  1061.4 221.6 reduce-scatter.13
  1288.6 225.3 reduce-scatter.7
  1521.2 276.1 reduce-scatter.9
  1803.7 276.5 reduce-scatter.11
where the time goes:
time: 2100 us; the launch traced here: 2090 us
  waiting for transfers between devices  1090 us (52%)
  blocking collectives  461 us (22%)
  matrix products  236 us (11%)
  other arithmetic  135 us (6%)
  local copies, waits for them, and re-layouts  134 us (6%)
    reduce_scatter x1, waiting for transfers between devices, shards(): lax.psum_scatter(expert_totals[0], 'dp', scatter_dimension=1, tiled=True)  283 us
    reduce_scatter x1, waiting for transfers between devices, shards(): lax.psum_scatter(expert_totals[1], 'dp', scatter_dimension=2, tiled=True)  283 us
    unnamed x2, blocking collectives  278 us
    reduce_scatter x1, waiting for transfers between devices, shards(): lax.psum_scatter(dense_totals[2], 'dp', scatter_dimension=0, tiled=True)  182 us
    all_gather x1, waiting for transfers between devices, shards(): lax.all_gather(expert_in[0], 'dp', axis=1, tiled=True)  95.2 us
    all_gather x1, blocking collectives, shards(): lax.all_gather(router[0], 'dp', axis=0, tiled=True)  92.6 us
    all_gather x1, blocking collectives, shards(): lax.all_gather(out_weight[0], 'dp', axis=1, tiled=True)  90.5 us
    another operation x36, other arithmetic, shards(): saved_stack = jax.tree.map(lambda *pieces: jnp.stack(pieces), *saved_list)  80.8 us
  transfers between devices with their start and end apart: 22, of which 18 were waited for; matrix products, arithmetic and copies ran while one was open for 10% of the time, Pallas kernels for 0%

commit v1 on v0

v1 whole, which is shorter than its diff:
```python
import jax
import jax.numpy as jnp
from jax import lax
from jax.sharding import Mesh
from jax.sharding import PartitionSpec as P

HEAD_DIM = 64
SEQ = 197
CAP = 128
EPS = 1e-06
PRECISE = lax.Precision.HIGHEST
F32 = jnp.float32
BF16 = jnp.bfloat16


def dot(a, b, dims, precision=None):
    return lax.dot_general(a, b, (dims, ((), ())), precision=precision, preferred_element_type=F32)


def swap(block, axis, distance=1):
    size = lax.axis_size(axis)
    return lax.ppermute(block, axis, [(i, i ^ distance) for i in range(size)])


def send_one_way(block, axis, source, target):
    return lax.ppermute(block, axis, [(source, target)])


def piece(blocks, index):
    return lax.dynamic_index_in_dim(blocks, index, 0, keepdims=False)


def gathered(block, axis, place=0):
    size = lax.axis_size(axis)
    own = lax.axis_index(axis)
    shape = block.shape[:place] + (size,) + block.shape[place:]
    total = jnp.zeros(shape, block.dtype)
    for distance in range(size):
        arrived = block if distance == 0 else swap(block, axis, distance)
        total = lax.dynamic_update_slice_in_dim(
            total, jnp.expand_dims(arrived, place), own ^ distance, place
        )
    return total


def scattered(blocks, axis):
    size = lax.axis_size(axis)
    own = lax.axis_index(axis)
    total = piece(blocks, own).astype(F32)
    for distance in range(1, size):
        total = total + swap(piece(blocks, own ^ distance), axis, distance).astype(F32)
    return total


def exchanged(blocks, axis):
    size = lax.axis_size(axis)
    return [blocks[k] if k == 0 else swap(blocks[k], axis, k) for k in range(size)]


def xor_order(blocks, index):
    paired = blocks.reshape((2, 2) + blocks.shape[1:])
    paired = jnp.where((index & 1) == 1, paired[:, ::-1], paired)
    paired = jnp.where((index & 2) == 2, paired[::-1], paired)
    return paired.reshape(blocks.shape)


def normalise(field):
    centered = field - jnp.mean(field, axis=-1, keepdims=True)
    scale = lax.rsqrt(jnp.mean(centered * centered, axis=-1, keepdims=True) + EPS)
    return centered * scale, scale


def norm_back(grad, unit, scale, gain):
    grad_unit = grad * gain[None, :]
    mean_grad = jnp.mean(grad_unit, axis=-1, keepdims=True)
    mean_cross = jnp.mean(grad_unit * unit, axis=-1, keepdims=True)
    grad_field = scale * (grad_unit - mean_grad - unit * mean_cross)
    return grad_field, jnp.sum(grad * unit, axis=0), jnp.sum(grad, axis=0)


def slot_table(route_ids, axis_x, mp_index):
    experts = lax.axis_size("x")
    tokens = route_ids.shape[0]
    order = jnp.arange(experts, dtype=jnp.int32) ^ axis_x
    named = jnp.any(route_ids.T[None, :, :] == order[:, None, None], axis=1)
    steps = jnp.arange(tokens, dtype=jnp.int32)
    earlier = (steps[:, None] < steps[None, :]).astype(BF16)
    position = dot(named.astype(BF16), earlier, ((1,), (0,))).astype(jnp.int32)
    slots = jnp.arange(CAP // 2, dtype=jnp.int32) + mp_index * (CAP // 2)
    return named[:, None, :] & (position[:, None, :] == slots[None, :, None])


def to_experts(half):
    own = jnp.concatenate(exchanged(half, "x"), axis=0)
    return jnp.concatenate([own, swap(own, "mp")], axis=0)


def from_experts(partial, experts):
    rows = partial.shape[0] // 2
    other = swap(partial[rows:].astype(BF16), "mp")
    own = (partial[:rows] + other.astype(F32)).astype(BF16)
    own = own.reshape(experts, rows // experts, -1)
    return jnp.concatenate(exchanged(own, "x"), axis=0)


def forward_layer(dense, experts_pair, tokens, table, axis_x):
    qkv, out_t, gain_one, shift_one, gain_two, shift_two, router = dense
    first, second = experts_pair
    count, width = tokens.shape
    experts = table.shape[0]
    half_width = out_t.shape[1]
    heads = half_width // HEAD_DIM
    unit_one, scale_one = normalise(tokens)
    normed_one = (unit_one * gain_one[None, :] + shift_one[None, :]).astype(BF16)
    projected = dot(normed_one, qkv, ((1,), (0,))).astype(BF16)
    parts = projected.reshape(count, 3, heads, HEAD_DIM)
    queries, keys_all, values_all = parts[:, 0], parts[:, 1], parts[:, 2]
    scores = jnp.einsum(
        "qhe,khe->hqk", queries, keys_all, preferred_element_type=F32
    ) * HEAD_DIM ** (-0.5)
    probability = jax.nn.softmax(scores, axis=-1)
    prob_low = probability.astype(BF16)
    mixed = (
        jnp.einsum("hqk,khe->qhe", prob_low, values_all, preferred_element_type=F32)
        .astype(BF16)
        .reshape(count, half_width)
    )
    attended = dot(mixed, out_t, ((1,), (1,)))
    attended = attended + swap(attended, "mp")
    hidden = tokens + attended
    unit_two, scale_two = normalise(hidden)
    normed_two = (unit_two * gain_two[None, :] + shift_two[None, :]).astype(BF16)
    gates = jax.nn.softmax(dot(router, normed_two, ((0,), (1,))), axis=0)
    select = table.astype(BF16).reshape(-1, count)
    slot_gates = jnp.sum(jnp.where(table, gates[:, None, :], 0.0), axis=2).reshape(-1, 1)
    dispatched = to_experts(
        dot(select, normed_two, ((1,), (0,))).astype(BF16).reshape(experts, -1, width)
    )
    inner_pre = dot(dispatched, first, ((1,), (0,)))
    activated = jax.nn.gelu(inner_pre, approximate=False).astype(BF16)
    expert_sum = from_experts(dot(activated, second, ((1,), (1,))), experts)
    weighted = (slot_gates * expert_sum.astype(F32)).astype(BF16)
    mixture = dot(select, weighted, ((0,), (0,)))
    output = hidden + (mixture + swap(mixture, "mp"))
    saved = (
        unit_one,
        scale_one,
        normed_one,
        queries,
        keys_all,
        values_all,
        probability,
        prob_low,
        mixed,
        unit_two,
        scale_two,
        normed_two,
        gates,
        table,
        select,
        slot_gates,
        dispatched,
        inner_pre,
        activated,
        expert_sum,
    )
    return output.astype(BF16), saved


def backward_layer(dense, experts_pair, saved, grad_low):
    qkv, out_t, gain_one, shift_one, gain_two, shift_two, router = dense
    first, second = experts_pair
    (
        unit_one,
        scale_one,
        normed_one,
        queries,
        keys_all,
        values_all,
        probability,
        prob_low,
        mixed,
        unit_two,
        scale_two,
        normed_two,
        gates,
        table,
        select,
        slot_gates,
        dispatched,
        inner_pre,
        activated,
        expert_sum,
    ) = saved
    experts = table.shape[0]
    count, width = grad_low.shape
    grad_output = grad_low.astype(F32)
    grad_slots = dot(select, grad_low, ((1,), (0,)))
    slot_chosen = jnp.sum(grad_slots * expert_sum.astype(F32), axis=1).reshape(experts, -1, 1)
    grad_gates = jnp.sum(jnp.where(table, slot_chosen, 0.0), axis=1)
    grad_gates = grad_gates + swap(grad_gates, "mp")
    grad_expert = to_experts(
        (slot_gates * grad_slots).astype(BF16).reshape(experts, -1, width)
    )
    grad_act = dot(grad_expert, second, ((1,), (0,)))
    unused, gelu_back = jax.vjp(lambda field: jax.nn.gelu(field, approximate=False), inner_pre)
    grad_inner = gelu_back(grad_act)[0].astype(BF16)
    grad_dispatched = from_experts(dot(grad_inner, first, ((1,), (1,))), experts)
    grad_second = dot(grad_expert, activated, ((0,), (0,))).astype(BF16)
    grad_first = dot(dispatched, grad_inner, ((0,), (0,))).astype(BF16)
    returned = dot(select, grad_dispatched, ((0,), (0,)))
    returned = returned + swap(returned, "mp")
    grad_logits = gates * (grad_gates - jnp.sum(gates * grad_gates, axis=0, keepdims=True))
    grad_router = dot(normed_two.astype(F32), grad_logits, ((0,), (1,)), PRECISE)
    grad_normed = returned + dot(grad_logits, router.astype(F32), ((0,), (1,)), PRECISE)
    grad_hidden, grad_gain_two, grad_shift_two = norm_back(
        grad_normed, unit_two, scale_two, gain_two
    )
    grad_hidden = grad_output + grad_hidden
    grad_attended = grad_hidden.astype(BF16)
    grad_out_t = dot(grad_attended, mixed, ((0,), (0,)))
    grad_mixed = dot(grad_attended, out_t, ((1,), (0,))).astype(BF16).reshape(queries.shape)
    grad_prob = jnp.einsum("qhe,khe->hqk", grad_mixed, values_all, preferred_element_type=F32)
    grad_values = jnp.einsum("hqk,qhe->khe", prob_low, grad_mixed, preferred_element_type=F32)
    grad_scores = (
        probability * (grad_prob - jnp.sum(probability * grad_prob, axis=-1, keepdims=True))
    ).astype(BF16)
    grad_queries = jnp.einsum(
        "hqk,khe->qhe", grad_scores, keys_all, preferred_element_type=F32
    ) * HEAD_DIM ** (-0.5)
    grad_keys = jnp.einsum(
        "hqk,qhe->khe", grad_scores, queries, preferred_element_type=F32
    ) * HEAD_DIM ** (-0.5)
    grad_projected = (
        jnp.stack([grad_queries, grad_keys, grad_values], axis=1).astype(BF16).reshape(count, -1)
    )
    grad_qkv = dot(normed_one, grad_projected, ((0,), (0,)))
    grad_normed = dot(grad_projected, qkv, ((1,), (1,)))
    grad_normed = grad_normed + swap(grad_normed, "mp")
    grad_tokens, grad_gain_one, grad_shift_one = norm_back(
        grad_normed, unit_one, scale_one, gain_one
    )
    vectors = jnp.stack([grad_gain_one, grad_shift_one, grad_gain_two, grad_shift_two], axis=1)
    dense_grads = (grad_qkv, grad_out_t, vectors, grad_router)
    return (grad_hidden + grad_tokens).astype(BF16), dense_grads, (grad_first, grad_second)


def shards(
    inputs,
    cotangent,
    routes,
    gain_one,
    shift_one,
    qkv_weight,
    out_weight,
    gain_two,
    shift_two,
    router,
    expert_in,
    expert_out,
):
    section = lax.axis_index("section")
    axis_x = lax.axis_index("x")
    mp_index = lax.axis_index("mp")
    size_g = lax.axis_size("g")
    size_x = lax.axis_size("x")
    rows = qkv_weight.shape[1]
    width = rows * size_g * size_x
    half_width = out_weight.shape[1]
    first_section = section == 0

    def by_layer(own):
        other = swap(own, "section")
        return jnp.where(first_section, own, other), jnp.where(first_section, other, own)

    small = jnp.stack([gain_one[0], shift_one[0], gain_two[0], shift_two[0]], axis=1)
    attention_shard = qkv_weight[0].reshape(rows, 3 * half_width)
    rest_shard = jnp.concatenate(
        [out_weight[0].T, small, router[0], jnp.zeros((rows, 120), BF16)], axis=1
    )
    expert_shard = jnp.stack([expert_in[0], jnp.swapaxes(expert_out[0], 1, 2)], axis=1)
    attention_pair = by_layer(attention_shard)
    rest_pair = by_layer(rest_shard)
    expert_pair = by_layer(expert_shard)
    routes_own = routes[0, :, 0]
    routes_kept = piece(routes_own, section)
    routes_other = swap(piece(routes_own, 1 - section), "section")
    routes_pair = (
        jnp.where(first_section, routes_kept, routes_other),
        jnp.where(first_section, routes_other, routes_kept),
    )

    def dense_weights(layer):
        qkv = gathered(gathered(attention_pair[layer], "x"), "g").reshape(width, -1)
        rest = gathered(gathered(rest_pair[layer], "g"), "x", 1).reshape(width, -1)
        out_t = rest[:, :half_width]
        extra = rest[:, half_width : half_width + 8]
        vectors = extra[:, :4].astype(F32).T
        router_here = xor_order(extra[:, 4:].T, axis_x).T
        return (qkv, out_t, vectors[0], vectors[1], vectors[2], vectors[3], router_here)

    def expert_weights(layer):
        shard = expert_pair[layer]
        own = lax.axis_index("x")
        ordered = jnp.zeros((2, size_x) + shard.shape[2:], BF16)
        for distance in range(size_x):
            mine = piece(shard, own ^ distance)
            if distance > 0:
                mine = swap(mine, "x", distance)
            ordered = lax.dynamic_update_slice_in_dim(
                ordered, jnp.expand_dims(mine, 1), own ^ distance, 1
            )
        ordered = ordered.reshape(2, size_x * rows, -1)
        return tuple(
            (gathered(ordered[i], "g").reshape(width, -1) for i in range(2))
        )

    dense = (dense_weights(0), dense_weights(1))
    experts_here = (expert_weights(0), expert_weights(1))
    tables = tuple((slot_table(r, axis_x, mp_index) for r in routes_pair))
    tokens = piece(inputs[:, 0], section)
    out_zero, saved_zero = forward_layer(
        dense[0], experts_here[0], tokens.astype(F32), tables[0], axis_x
    )
    out_one, saved_one = forward_layer(
        dense[1], experts_here[1], out_zero.astype(F32), tables[1], axis_x
    )

    def by_section(zero, one):
        to_first = send_one_way(zero, "section", 1, 0)
        to_second = send_one_way(one, "section", 0, 1)
        low = jnp.where(first_section, zero, to_second)
        high = jnp.where(first_section, to_first, one)
        return jnp.stack([low, high])[None, :, None]

    acts = by_section(out_zero, out_one)

    def reduced_experts(layer, grads):
        first, second = grads
        parts = []
        for member in (first, second):
            parts.append(scattered(member.reshape(size_g, size_x * rows, -1), "g").astype(BF16))
        both = jnp.stack(parts).reshape(2, size_x, rows, -1)
        arrived = []
        for distance in range(size_x):
            mine = lax.dynamic_index_in_dim(both, axis_x ^ distance, 1, keepdims=False)
            arrived.append(mine if distance == 0 else swap(mine, "x", distance))
        arrived = xor_order(jnp.stack(arrived), axis_x)
        other = send_one_way(arrived, "section", 1 - layer, layer)
        return arrived.astype(F32) + other.astype(F32)

    def reduced_dense(layer, grads):
        grad_qkv, grad_out_t, vectors, grad_router = grads
        grad_router = xor_order(grad_router.T, axis_x).T
        rest = jnp.concatenate(
            [grad_out_t, vectors, grad_router, jnp.zeros((width, 120), F32)], axis=1
        ).astype(BF16)
        low = grad_qkv.astype(BF16).reshape(size_g, size_x * rows, -1)
        low = scattered(low, "g").astype(BF16)
        low = scattered(low.reshape(size_x, rows, -1), "x")
        rest = jnp.swapaxes(rest.reshape(size_g, size_x, rows, -1), 0, 1)
        rest = scattered(rest, "x").astype(BF16)
        rest = scattered(rest, "g")
        total = jnp.concatenate([low, rest], axis=1)
        other = send_one_way(total, "section", 1 - layer, layer)
        return total + other

    grad_mid, dense_one, expert_one = backward_layer(
        dense[1], experts_here[1], saved_one, piece(cotangent[:, 0], section)
    )
    experts_sum_one = reduced_experts(1, expert_one)
    dense_sum_one = reduced_dense(1, dense_one)
    grad_in, dense_zero, expert_zero = backward_layer(
        dense[0], experts_here[0], saved_zero, grad_mid
    )
    experts_sum_zero = reduced_experts(0, expert_zero)
    dense_sum_zero = reduced_dense(0, dense_zero)
    input_grads = by_section(grad_in, grad_mid)
    expert_sum = jnp.where(first_section, experts_sum_zero, experts_sum_one)
    dense_sum = jnp.where(first_section, dense_sum_zero, dense_sum_one)
    grad_first = expert_sum[:, 0]
    grad_second = jnp.swapaxes(expert_sum[:, 1], 1, 2)
    full = 3 * half_width
    grad_qkv = dense_sum[:, :full].reshape(rows, 3, half_width)
    grad_out = dense_sum[:, full : full + half_width].T
    tail = dense_sum[:, full + half_width :]
    outs = (
        tail[:, 0],
        tail[:, 1],
        grad_qkv,
        grad_out,
        tail[:, 2],
        tail[:, 3],
        tail[:, 4:8],
        grad_first,
        grad_second,
    )
    return (acts, input_grads) + tuple((member[None] for member in outs))


def solution(mesh):
    sections, batch, pair = mesh.devices.shape
    inner = Mesh(mesh.devices.reshape(sections, batch // 4, 4, pair), ("section", "g", "x", "mp"))
    dp = ("g", "x")
    placed = (
        P(None, dp, None, None),
        P(None, dp, None, None),
        P("section", None, dp, None, None),
        P("section", dp),
        P("section", dp),
        P("section", dp, None, "mp"),
        P("section", "mp", dp),
        P("section", dp),
        P("section", dp),
        P("section", dp, None),
        P("section", None, dp, "mp"),
        P("section", None, "mp", dp),
    )
    return jax.shard_map(
        shards,
        mesh=inner,
        in_specs=placed,
        out_specs=(
            P("section", None, dp, None, None),
            P("section", None, dp, None, None),
            P("section", dp),
            P("section", dp),
            P("section", dp, None, "mp"),
            P("section", "mp", dp),
            P("section", dp),
            P("section", dp),
            P("section", dp, None),
            P("section", None, dp, "mp"),
            P("section", None, "mp", dp),
        ),
        check_vma=False,
    )
```

time: 2100 us -> 784 us (0.37)
  waiting for transfers between devices: 1090 us -> 217 us
  blocking collectives: 461 us -> 0 us
  starting transfers between devices: 11.6 us -> 345 us
  matrix products: 236 us -> 75.9 us
  other arithmetic: 135 us -> 34.1 us
  local copies, waits for them, and re-layouts: 134 us -> 95.9 us
    reduce_scatter x3 -> x0, waiting for transfers between devices: 748 us -> none  [the longest x1 283 us: shards(): lax.psum_scatter(expert_totals[0], 'dp', scatter_dimension=1, tiled=True)]
    ppermute x4 -> x202, starting transfers between devices: 8.98 us -> 345 us  [the longest x194 326 us: swap(): return lax.ppermute(block, axis, [(i, i ^ distance) for i in range(size)])]
    unnamed x2 -> x0, blocking collectives: 278 us -> none
    psum x11 -> x0, waiting for transfers between devices: 195 us -> none  [the longest x3 51.5 us: backward_dense(): lax.psum(jnp.einsum('tcf,dcf->td', grad_projected, qkv_matrix, preferred_...]
    ppermute x4 -> x202, waiting for transfers between devices: 24.5 us -> 217 us  [the longest x194 210 us: swap(): return lax.ppermute(block, axis, [(i, i ^ distance) for i in range(size)])]
    all_gather x2 -> x0, blocking collectives: 183 us -> none  [the longest x1 92.6 us: shards(): lax.all_gather(router[0], 'dp', axis=0, tiled=True)]
    dot_general x66 -> x50, matrix products: 231 us -> 72.7 us  [the longest x40 63.7 us: dot(): lax.dot_general(a, b, (dims, ((), ())), precision=precision, preferred_el...]
    all_gather x3 -> x0, waiting for transfers between devices: 122 us -> none  [the longest x1 95.2 us: shards(): lax.all_gather(expert_in[0], 'dp', axis=1, tiled=True)]
  transfers between devices with their start and end apart: 22 -> 202, of which waited for: 18 -> 67; matrix products, arithmetic and copies ran while one was open for 10% -> 20% of each run, Pallas kernels for 0% -> 0%
where the time goes in v1:
time: 784 us; the launch traced here: 772 us
  starting transfers between devices  345 us (44%)
  waiting for transfers between devices  217 us (28%)
  local copies, waits for them, and re-layouts  95.9 us (12%)
  matrix products  75.9 us (10%)
  other arithmetic  34.1 us (4%)
    ppermute x194, starting transfers between devices, swap(): return lax.ppermute(block, axis, [(i, i ^ distance) for i in range(size)])  326 us
    ppermute x194, waiting for transfers between devices, swap(): return lax.ppermute(block, axis, [(i, i ^ distance) for i in range(size)])  210 us
    dot_general x40, matrix products, dot(): lax.dot_general(a, b, (dims, ((), ())), precision=precision, preferred_el...  63.7 us
    dynamic_update_slice x75, local copies, waits for them, and re-layouts, gathered(): lax.dynamic_update_slice_in_dim(total, jnp.expand_dims(arrived, place), o...  27.1 us
    ppermute x8, starting transfers between devices, send_one_way(): return lax.ppermute(block, axis, [(source, target)])  18.9 us
    unnamed x299, local copies, waits for them, and re-layouts  17.6 us
  transfers between devices with their start and end apart: 202, of which 67 were waited for; matrix products, arithmetic and copies ran while one was open for 20% of the time, Pallas kernels for 0%

profile of v1, /device:TPU:16, one launch (start us, length us, event | category | flops | bytes accessed | tf_op | source)
XLA Modules:
  0.0 771.6 jit_solution(11883290385438791594)
XLA Ops:
  56.5 6.4 collective-permute-start.6
  125.9 5.3 collective-permute-start.20
  158.1 5.9 collective-permute-start.70
  201.3 5.5 collective-permute-start.44
  225.5 6.3 collective-permute-start.37
  231.8 4.7 collective-permute-start.38
  236.6 5.0 collective-permute-start.80
  251.7 15.5 %collective-permute-done.80 = bf16[96,1536]{1,0:T(8,128)(2,1)S(1)} collective-permute-done((bf16[96,1536]{1,0:T(8,128)(2,1)S(1)}, bf16[96,1536]{1,0:T(8,128)(2,1)S(1)}, u32[]{:S(2)}, u32[]{:S(2)}) %collective-permute-start.80) | collective-permute-done | bytes 294944 | tf_op jit(solution)/shard_map/ppermute | solution.py:22
  283.0 9.9 %multiply_convert_fusion.1 = (bf16[512,1536]{1,0:T(8,128)(2,1)S(1)}, f32[512,1536]{1,0:T(8,128)}, f32[512,1536]{1,0:T(8,128)}) fusion(bf16[512,768]{1,0:T(8,128)(2,1)S(1)} %constant_dynamic-update-slice_fusion.20, bf16[768,1536]{1,0:T(8,128)(2,1)S(1)} %bitcast.737), kind=kOutput, calls=%fused_computation.27 | convolution fusion | flops 1259077632 | bytes 11010048 | tf_op jit(solution)/shard_map/dot_general | solution.py:17
  307.2 4.3 collective-permute-start.91
  338.7 9.7 %multiply_convert_fusion = (bf16[512,1536]{1,0:T(8,128)(2,1)S(1)}, f32[512,1536]{1,0:T(8,128)}, f32[512,1536]{1,0:T(8,128)}) fusion(bf16[512,768]{1,0:T(8,128)(2,1)S(1)} %constant_dynamic-update-slice_fusion.25, bf16[768,1536]{1,0:T(8,128)(2,1)S(1)} %bitcast.739), kind=kOutput, calls=%fused_computation.14 | convolution fusion | flops 1259077632 | bytes 11010048 | tf_op jit(solution)/shard_map/dot_general | solution.py:17
  399.0 4.5 collective-permute-start.196
  403.5 14.2 %collective-permute-done.192 = bf16[96,1536]{1,0:T(8,128)(2,1)S(1)} collective-permute-done((bf16[96,1536]{1,0:T(8,128)(2,1)S(1)}, bf16[96,1536]{1,0:T(8,128)(2,1)S(1)}, u32[]{:S(2)}, u32[]{:S(2)}) %collective-permute-start.192) | collective-permute-done | bytes 294944 | tf_op jit(solution)/shard_map/ppermute | solution.py:22
  422.0 4.7 collective-permute-start.186
  435.6 8.5 %collective-permute-done.185 = bf16[96,1536]{1,0:T(8,128)(2,1)S(1)} collective-permute-done((bf16[96,1536]{1,0:T(8,128)(2,1)S(1)}, bf16[96,1536]{1,0:T(8,128)(2,1)S(1)}, u32[]{:S(2)}, u32[]{:S(2)}) %collective-permute-start.185) | collective-permute-done | bytes 294944 | tf_op jit(solution)/shard_map/ppermute | solution.py:22
  450.0 8.0 %collective-permute-done.190 = bf16[96,1536]{1,0:T(8,128)(2,1)S(1)} collective-permute-done((bf16[96,1536]{1,0:T(8,128)(2,1)S(1)}, bf16[96,1536]{1,0:T(8,128)(2,1)S(1)}, u32[]{:S(2)}, u32[]{:S(2)}) %collective-permute-start.190) | collective-permute-done | bytes 294944 | tf_op jit(solution)/shard_map/ppermute | solution.py:22
  458.7 4.5 collective-permute-start.200
  470.5 4.4 collective-permute-done.107
  489.1 4.7 collective-permute-start.147
  497.4 4.6 collective-permute-start.150
  573.9 4.5 collective-permute-start.178
  578.4 14.7 %collective-permute-done.174 = bf16[96,1536]{1,0:T(8,128)(2,1)S(1)} collective-permute-done((bf16[96,1536]{1,0:T(8,128)(2,1)S(1)}, bf16[96,1536]{1,0:T(8,128)(2,1)S(1)}, u32[]{:S(2)}, u32[]{:S(2)}) %collective-permute-start.174) | collective-permute-done | bytes 294944 | tf_op jit(solution)/shard_map/ppermute | solution.py:22
  602.8 5.1 collective-permute-done.179
  610.2 12.7 %collective-permute-done.167 = bf16[96,1536]{1,0:T(8,128)(2,1)S(1)} collective-permute-done((bf16[96,1536]{1,0:T(8,128)(2,1)S(1)}, bf16[96,1536]{1,0:T(8,128)(2,1)S(1)}, u32[]{:S(2)}, u32[]{:S(2)}) %collective-permute-start.167) | collective-permute-done | bytes 294944 | tf_op jit(solution)/shard_map/ppermute | solution.py:22
  626.5 10.0 %collective-permute-done.172 = bf16[96,1536]{1,0:T(8,128)(2,1)S(1)} collective-permute-done((bf16[96,1536]{1,0:T(8,128)(2,1)S(1)}, bf16[96,1536]{1,0:T(8,128)(2,1)S(1)}, u32[]{:S(2)}, u32[]{:S(2)}) %collective-permute-start.172) | collective-permute-done | bytes 294944 | tf_op jit(solution)/shard_map/ppermute | solution.py:22
  648.9 4.8 collective-permute-start.163
  688.2 5.4 collective-permute-start.129
  699.1 5.9 collective-permute-start.122
  705.0 4.6 collective-permute-done.130
  744.6 5.3 collective-permute-start.142
  752.8 5.0 collective-permute-start.165
  760.6 5.9 collective-permute-done.123
  (1015 shorter events, 546.6 us)
Async XLA Ops:
  2.7 165.2 %collective-permute-start.28 = (bf16[4,2,24,1536]{3,2,0,1:T(8,128)(2,1)}, bf16[4,2,24,1536]{3,2,0,1:T(8,128)(2,1)}, u32[]{:S(2)}, u32[]{:S(2)}) collective-permute-start(bf16[4,2,24,1536]{3,2,0,1:T(8,128)(2,1)} %pad_maximum_fusion), channel_id=1, source_target_pairs={{0,64},{64,0},{1,65},{65,1},{2,66},{66,2},{3,67},{67,3},{4,68},{68... | collective-permute-start | bytes 1769480 | tf_op jit(solution)/shard_map/ppermute | solution.py:22
  10.2 61.9 %collective-permute-start.11 = (bf16[24,1152]{1,0:T(8,128)(2,1)S(1)}, bf16[24,1152]{1,0:T(8,128)(2,1)S(1)}, u32[]{:S(2)}, u32[]{:S(2)}) collective-permute-start(bf16[24,1152]{1,0:T(8,128)(2,1)S(1)} %bitcast.811), channel_id=1, source_target_pairs={{0,64},{64,0},{1,65},{65,1},{2,66},{66,2},{3,67},{67,3},{4,68},{68... | collective-permute-start | bytes 165896 | tf_op jit(solution)/shard_map/ppermute | solution.py:22
  63.9 41.1 %collective-permute-start.58 = (bf16[8,24,512]{2,1,0:T(8,128)(2,1)S(1)}, bf16[8,24,512]{2,1,0:T(8,128)(2,1)S(1)}, u32[]{:S(2)}, u32[]{:S(2)}) collective-permute-start(bf16[8,24,512]{2,1,0:T(8,128)(2,1)S(1)} %constant_dynamic-update-slice_fusion.2), channel_id=1, source_target_pairs={{0,2},{2,0},{4,6},{6,4},{1,3},{3,1},{5,7},{7,5},{8,10},{10,8},{12,... | collective-permute-start | bytes 589832 | tf_op jit(solution)/shard_map/ppermute | solution.py:22
  65.4 41.6 %collective-permute-start.59 = (bf16[8,24,512]{2,1,0:T(8,128)(2,1)S(1)}, bf16[8,24,512]{2,1,0:T(8,128)(2,1)S(1)}, u32[]{:S(2)}, u32[]{:S(2)}) collective-permute-start(bf16[8,24,512]{2,1,0:T(8,128)(2,1)S(1)} %constant_dynamic-update-slice_fusion.2), channel_id=1, source_target_pairs={{0,4},{2,6},{4,0},{6,2},{1,5},{3,7},{5,1},{7,3},{8,12},{10,14},{12... | collective-permute-start | bytes 589832 | tf_op jit(solution)/shard_map/ppermute | solution.py:22
  70.4 38.1 %collective-permute-start.8 = (bf16[8,24,512]{2,1,0:T(8,128)(2,1)S(1)}, bf16[8,24,512]{2,1,0:T(8,128)(2,1)S(1)}, u32[]{:S(2)}, u32[]{:S(2)}) collective-permute-start(bf16[8,24,512]{2,1,0:T(8,128)(2,1)S(1)} %constant_dynamic-update-slice_fusion.12), channel_id=1, source_target_pairs={{0,2},{2,0},{4,6},{6,4},{1,3},{3,1},{5,7},{7,5},{8,10},{10,8},{12,... | collective-permute-start | bytes 589832 | tf_op jit(solution)/shard_map/ppermute | solution.py:22
  165.4 31.5 %collective-permute-start.22 = (f32[197,768]{1,0:T(8,128)S(1)}, f32[197,768]{1,0:T(8,128)S(1)}, u32[]{:S(2)}, u32[]{:S(2)}) collective-permute-start(f32[197,768]{1,0:T(8,128)S(1)} %fusion.98), channel_id=1, source_target_pairs={{0,1},{1,0},{2,3},{3,2},{4,5},{5,4},{6,7},{7,6},{8,9},{9,8},{10,11... | collective-permute-start | bytes 1815560 | tf_op jit(solution)/shard_map/ppermute | solution.py:22
  188.0 24.4 %collective-permute-start.41 = (bf16[96,1536]{1,0:T(8,128)(2,1)}, bf16[96,1536]{1,0:T(8,128)(2,1)}, u32[]{:S(2)}, u32[]{:S(2)}) collective-permute-start(bf16[96,1536]{1,0:T(8,128)(2,1)} %bitcast.73), channel_id=1, source_target_pairs={{0,24},{8,16},{16,8},{24,0},{32,56},{40,48},{48,40},{56,32},{1,25}... | collective-permute-start | bytes 884744 | tf_op jit(solution)/shard_map/ppermute | solution.py:22
  236.6 30.5 %collective-permute-start.80 = (bf16[96,1536]{1,0:T(8,128)(2,1)S(1)}, bf16[96,1536]{1,0:T(8,128)(2,1)S(1)}, u32[]{:S(2)}, u32[]{:S(2)}) collective-permute-start(bf16[96,1536]{1,0:T(8,128)(2,1)S(1)} %bitcast.783), channel_id=1, source_target_pairs={{0,16},{8,24},{16,0},{24,8},{32,48},{40,56},{48,32},{56,40},{1,17}... | collective-permute-start | bytes 884744 | tf_op jit(solution)/shard_map/ppermute | solution.py:22
  241.6 28.9 %collective-permute-start.81 = (bf16[96,1536]{1,0:T(8,128)(2,1)S(1)}, bf16[96,1536]{1,0:T(8,128)(2,1)S(1)}, u32[]{:S(2)}, u32[]{:S(2)}) collective-permute-start(bf16[96,1536]{1,0:T(8,128)(2,1)S(1)} %bitcast.784), channel_id=1, source_target_pairs={{0,24},{8,16},{16,8},{24,0},{32,56},{40,48},{48,40},{56,32},{1,25}... | collective-permute-start | bytes 884744 | tf_op jit(solution)/shard_map/ppermute | solution.py:22
  242.5 28.2 %collective-permute-start.82 = (bf16[96,1536]{1,0:T(8,128)(2,1)S(1)}, bf16[96,1536]{1,0:T(8,128)(2,1)S(1)}, u32[]{:S(2)}, u32[]{:S(2)}) collective-permute-start(bf16[96,1536]{1,0:T(8,128)(2,1)S(1)} %bitcast.785), channel_id=1, source_target_pairs={{0,32},{8,40},{16,48},{24,56},{32,0},{40,8},{48,16},{56,24},{1,33}... | collective-permute-start | bytes 884744 | tf_op jit(solution)/shard_map/ppermute | solution.py:22
  247.2 25.9 %collective-permute-start.83 = (bf16[96,1536]{1,0:T(8,128)(2,1)S(1)}, bf16[96,1536]{1,0:T(8,128)(2,1)S(1)}, u32[]{:S(2)}, u32[]{:S(2)}) collective-permute-start(bf16[96,1536]{1,0:T(8,128)(2,1)S(1)} %bitcast.786), channel_id=1, source_target_pairs={{0,40},{8,32},{16,56},{24,48},{32,8},{40,0},{48,24},{56,16},{1,41}... | collective-permute-start | bytes 884744 | tf_op jit(solution)/shard_map/ppermute | solution.py:22
  247.9 33.2 %collective-permute-start.84 = (bf16[96,1536]{1,0:T(8,128)(2,1)S(1)}, bf16[96,1536]{1,0:T(8,128)(2,1)S(1)}, u32[]{:S(2)}, u32[]{:S(2)}) collective-permute-start(bf16[96,1536]{1,0:T(8,128)(2,1)S(1)} %bitcast.787), channel_id=1, source_target_pairs={{0,48},{8,56},{16,32},{24,40},{32,16},{40,24},{48,0},{56,8},{1,49}... | collective-permute-start | bytes 884744 | tf_op jit(solution)/shard_map/ppermute | solution.py:22
  267.1 27.7 %collective-permute-start.85 = (bf16[96,1536]{1,0:T(8,128)(2,1)S(1)}, bf16[96,1536]{1,0:T(8,128)(2,1)S(1)}, u32[]{:S(2)}, u32[]{:S(2)}) collective-permute-start(bf16[96,1536]{1,0:T(8,128)(2,1)S(1)} %bitcast.788), channel_id=1, source_target_pairs={{0,56},{8,48},{16,40},{24,32},{32,24},{40,16},{48,8},{56,0},{1,57}... | collective-permute-start | bytes 884744 | tf_op jit(solution)/shard_map/ppermute | solution.py:22
  276.1 24.1 %collective-permute-start.86 = (bf16[96,1536]{1,0:T(8,128)(2,1)S(1)}, bf16[96,1536]{1,0:T(8,128)(2,1)S(1)}, u32[]{:S(2)}, u32[]{:S(2)}) collective-permute-start(bf16[96,1536]{1,0:T(8,128)(2,1)S(1)} %bitcast.774), channel_id=1, source_target_pairs={{0,8},{8,0},{16,24},{24,16},{32,40},{40,32},{48,56},{56,48},{1,9},... | collective-permute-start | bytes 884744 | tf_op jit(solution)/shard_map/ppermute | solution.py:22
  277.8 34.1 %collective-permute-start.87 = (bf16[96,1536]{1,0:T(8,128)(2,1)S(1)}, bf16[96,1536]{1,0:T(8,128)(2,1)S(1)}, u32[]{:S(2)}, u32[]{:S(2)}) collective-permute-start(bf16[96,1536]{1,0:T(8,128)(2,1)S(1)} %bitcast.775), channel_id=1, source_target_pairs={{0,16},{8,24},{16,0},{24,8},{32,48},{40,56},{48,32},{56,40},{1,17}... | collective-permute-start | bytes 884744 | tf_op jit(solution)/shard_map/ppermute | solution.py:22
  279.3 33.3 %collective-permute-start.88 = (bf16[96,1536]{1,0:T(8,128)(2,1)S(1)}, bf16[96,1536]{1,0:T(8,128)(2,1)S(1)}, u32[]{:S(2)}, u32[]{:S(2)}) collective-permute-start(bf16[96,1536]{1,0:T(8,128)(2,1)S(1)} %bitcast.776), channel_id=1, source_target_pairs={{0,24},{8,16},{16,8},{24,0},{32,56},{40,48},{48,40},{56,32},{1,25}... | collective-permute-start | bytes 884744 | tf_op jit(solution)/shard_map/ppermute | solution.py:22
  312.7 24.2 %collective-permute-start.92 = (bf16[96,1536]{1,0:T(8,128)(2,1)S(1)}, bf16[96,1536]{1,0:T(8,128)(2,1)}, u32[]{:S(2)}, u32[]{:S(2)}) collective-permute-start(bf16[96,1536]{1,0:T(8,128)(2,1)S(1)} %bitcast.780), channel_id=1, source_target_pairs={{0,56},{8,48},{16,40},{24,32},{32,24},{40,16},{48,8},{56,0},{1,57}... | collective-permute-start | bytes 884744 | tf_op jit(solution)/shard_map/ppermute | solution.py:22
  352.0 43.2 %collective-permute-start.99 = (bf16[197,768]{1,0:T(8,128)(2,1)S(1)}, bf16[197,768]{1,0:T(8,128)(2,1)}, u32[]{:S(2)}, u32[]{:S(2)}) collective-permute-start(bf16[197,768]{1,0:T(8,128)(2,1)S(1)} %get-tuple-element.106), channel_id=1, source_target_pairs={{64,0},{65,1},{66,2},{67,3},{68,4},{69,5},{70,6},{71,7},{72,8},{73... | collective-permute-start | bytes 907784 | tf_op jit(solution)/shard_map/ppermute | solution.py:26
  388.3 29.4 %collective-permute-start.192 = (bf16[96,1536]{1,0:T(8,128)(2,1)S(1)}, bf16[96,1536]{1,0:T(8,128)(2,1)S(1)}, u32[]{:S(2)}, u32[]{:S(2)}) collective-permute-start(bf16[96,1536]{1,0:T(8,128)(2,1)S(1)} %get-tuple-element.141), channel_id=1, source_target_pairs={{0,16},{8,24},{16,0},{24,8},{32,48},{40,56},{48,32},{56,40},{1,17}... | collective-permute-start | bytes 884744 | tf_op jit(solution)/shard_map/ppermute | solution.py:22
  392.1 26.7 %collective-permute-start.193 = (bf16[96,1536]{1,0:T(8,128)(2,1)S(1)}, bf16[96,1536]{1,0:T(8,128)(2,1)S(1)}, u32[]{:S(2)}, u32[]{:S(2)}) collective-permute-start(bf16[96,1536]{1,0:T(8,128)(2,1)S(1)} %get-tuple-element.140), channel_id=1, source_target_pairs={{0,24},{8,16},{16,8},{24,0},{32,56},{40,48},{48,40},{56,32},{1,25}... | collective-permute-start | bytes 884744 | tf_op jit(solution)/shard_map/ppermute | solution.py:22
  399.0 27.7 %collective-permute-start.196 = (bf16[96,1536]{1,0:T(8,128)(2,1)S(1)}, bf16[96,1536]{1,0:T(8,128)(2,1)S(1)}, u32[]{:S(2)}, u32[]{:S(2)}) collective-permute-start(bf16[96,1536]{1,0:T(8,128)(2,1)S(1)} %get-tuple-element.137), channel_id=1, source_target_pairs={{0,48},{8,56},{16,32},{24,40},{32,16},{40,24},{48,0},{56,8},{1,49}... | collective-permute-start | bytes 884744 | tf_op jit(solution)/shard_map/ppermute | solution.py:22
  418.9 25.3 %collective-permute-start.185 = (bf16[96,1536]{1,0:T(8,128)(2,1)S(1)}, bf16[96,1536]{1,0:T(8,128)(2,1)S(1)}, u32[]{:S(2)}, u32[]{:S(2)}) collective-permute-start(bf16[96,1536]{1,0:T(8,128)(2,1)S(1)} %get-tuple-element.148), channel_id=1, source_target_pairs={{0,16},{8,24},{16,0},{24,8},{32,48},{40,56},{48,32},{56,40},{1,17}... | collective-permute-start | bytes 884744 | tf_op jit(solution)/shard_map/ppermute | solution.py:22
  563.6 29.5 %collective-permute-start.174 = (bf16[96,1536]{1,0:T(8,128)(2,1)S(1)}, bf16[96,1536]{1,0:T(8,128)(2,1)S(1)}, u32[]{:S(2)}, u32[]{:S(2)}) collective-permute-start(bf16[96,1536]{1,0:T(8,128)(2,1)S(1)} %get-tuple-element.127), channel_id=1, source_target_pairs={{0,16},{8,24},{16,0},{24,8},{32,48},{40,56},{48,32},{56,40},{1,17}... | collective-permute-start | bytes 884744 | tf_op jit(solution)/shard_map/ppermute | solution.py:22
  567.2 28.0 %collective-permute-start.175 = (bf16[96,1536]{1,0:T(8,128)(2,1)S(1)}, bf16[96,1536]{1,0:T(8,128)(2,1)S(1)}, u32[]{:S(2)}, u32[]{:S(2)}) collective-permute-start(bf16[96,1536]{1,0:T(8,128)(2,1)S(1)} %get-tuple-element.126), channel_id=1, source_target_pairs={{0,24},{8,16},{16,8},{24,0},{32,56},{40,48},{48,40},{56,32},{1,25}... | collective-permute-start | bytes 884744 | tf_op jit(solution)/shard_map/ppermute | solution.py:22
  567.4 27.7 %collective-permute-start.176 = (bf16[96,1536]{1,0:T(8,128)(2,1)S(1)}, bf16[96,1536]{1,0:T(8,128)(2,1)S(1)}, u32[]{:S(2)}, u32[]{:S(2)}) collective-permute-start(bf16[96,1536]{1,0:T(8,128)(2,1)S(1)} %get-tuple-element.125), channel_id=1, source_target_pairs={{0,32},{8,40},{16,48},{24,56},{32,0},{40,8},{48,16},{56,24},{1,33}... | collective-permute-start | bytes 884744 | tf_op jit(solution)/shard_map/ppermute | solution.py:22
  569.6 29.6 %collective-permute-start.177 = (bf16[96,1536]{1,0:T(8,128)(2,1)S(1)}, bf16[96,1536]{1,0:T(8,128)(2,1)S(1)}, u32[]{:S(2)}, u32[]{:S(2)}) collective-permute-start(bf16[96,1536]{1,0:T(8,128)(2,1)S(1)} %get-tuple-element.124), channel_id=1, source_target_pairs={{0,40},{8,32},{16,56},{24,48},{32,8},{40,0},{48,24},{56,16},{1,41}... | collective-permute-start | bytes 884744 | tf_op jit(solution)/shard_map/ppermute | solution.py:22
  573.9 27.6 %collective-permute-start.178 = (bf16[96,1536]{1,0:T(8,128)(2,1)S(1)}, bf16[96,1536]{1,0:T(8,128)(2,1)S(1)}, u32[]{:S(2)}, u32[]{:S(2)}) collective-permute-start(bf16[96,1536]{1,0:T(8,128)(2,1)S(1)} %get-tuple-element.123), channel_id=1, source_target_pairs={{0,48},{8,56},{16,32},{24,40},{32,16},{40,24},{48,0},{56,8},{1,49}... | collective-permute-start | bytes 884744 | tf_op jit(solution)/shard_map/ppermute | solution.py:22
  595.2 27.8 %collective-permute-start.167 = (bf16[96,1536]{1,0:T(8,128)(2,1)S(1)}, bf16[96,1536]{1,0:T(8,128)(2,1)S(1)}, u32[]{:S(2)}, u32[]{:S(2)}) collective-permute-start(bf16[96,1536]{1,0:T(8,128)(2,1)S(1)} %get-tuple-element.134), channel_id=1, source_target_pairs={{0,16},{8,24},{16,0},{24,8},{32,48},{40,56},{48,32},{56,40},{1,17}... | collective-permute-start | bytes 884744 | tf_op jit(solution)/shard_map/ppermute | solution.py:22
  599.2 25.7 %collective-permute-start.168 = (bf16[96,1536]{1,0:T(8,128)(2,1)S(1)}, bf16[96,1536]{1,0:T(8,128)(2,1)S(1)}, u32[]{:S(2)}, u32[]{:S(2)}) collective-permute-start(bf16[96,1536]{1,0:T(8,128)(2,1)S(1)} %get-tuple-element.133), channel_id=1, source_target_pairs={{0,24},{8,16},{16,8},{24,0},{32,56},{40,48},{48,40},{56,32},{1,25}... | collective-permute-start | bytes 884744 | tf_op jit(solution)/shard_map/ppermute | solution.py:22
  601.5 24.8 %collective-permute-start.169 = (bf16[96,1536]{1,0:T(8,128)(2,1)S(1)}, bf16[96,1536]{1,0:T(8,128)(2,1)S(1)}, u32[]{:S(2)}, u32[]{:S(2)}) collective-permute-start(bf16[96,1536]{1,0:T(8,128)(2,1)S(1)} %get-tuple-element.132), channel_id=1, source_target_pairs={{0,32},{8,40},{16,48},{24,56},{32,0},{40,8},{48,16},{56,24},{1,33}... | collective-permute-start | bytes 884744 | tf_op jit(solution)/shard_map/ppermute | solution.py:22
  624.9 43.6 %collective-permute-start.201 = (bf16[4,2,24,1536]{3,2,0,1:T(8,128)(2,1)S(1)}, bf16[4,2,24,1536]{3,2,0,1:T(8,128)(2,1)S(1)}, u32[]{:S(2)}, u32[]{:S(2)}) collective-permute-start(bf16[4,2,24,1536]{3,2,0,1:T(8,128)(2,1)S(1)} %bitcast.753), channel_id=1, source_target_pairs={{0,64},{1,65},{2,66},{3,67},{4,68},{5,69},{6,70},{7,71},{8,72},{9,... | collective-permute-start | bytes 1769480 | tf_op jit(solution)/shard_map/ppermute | solution.py:26
  699.1 45.3 %collective-permute-start.122 = (bf16[197,768]{1,0:T(8,128)(2,1)S(1)}, bf16[197,768]{1,0:T(8,128)(2,1)}, u32[]{:S(2)}, u32[]{:S(2)}) collective-permute-start(bf16[197,768]{1,0:T(8,128)(2,1)S(1)} %fusion.52), channel_id=1, source_target_pairs={{0,64},{1,65},{2,66},{3,67},{4,68},{5,69},{6,70},{7,71},{8,72},{9,... | collective-permute-start | bytes 907784 | tf_op jit(solution)/shard_map/ppermute | solution.py:26
  (311 other events, 4029.3 us)

commit v2 on v1

v2 whole, which is shorter than its diff:
```python
import jax
import jax.numpy as jnp
from jax import lax
from jax.sharding import Mesh
from jax.sharding import PartitionSpec as P

HEAD_DIM = 64
SEQ = 197
CAP = 128
EPS = 1e-06
PRECISE = lax.Precision.HIGHEST
F32 = jnp.float32
BF16 = jnp.bfloat16


def dot(a, b, dims, precision=None):
    return lax.dot_general(a, b, (dims, ((), ())), precision=precision, preferred_element_type=F32)


def swap(block, axis, distance=1):
    size = lax.axis_size(axis)
    return lax.ppermute(block, axis, [(i, i ^ distance) for i in range(size)])


def piece(blocks, index):
    return lax.dynamic_index_in_dim(blocks, index, 0, keepdims=False)


def all_to_all(blocks, axis):
    return lax.all_to_all(blocks, axis, 0, 0, tiled=True)


def summed(blocks):
    return jnp.sum(blocks.astype(F32), axis=0)


def normalise(field):
    centered = field - jnp.mean(field, axis=-1, keepdims=True)
    scale = lax.rsqrt(jnp.mean(centered * centered, axis=-1, keepdims=True) + EPS)
    return centered * scale, scale


def norm_back(grad, unit, scale, gain):
    grad_unit = grad * gain[None, :]
    mean_grad = jnp.mean(grad_unit, axis=-1, keepdims=True)
    mean_cross = jnp.mean(grad_unit * unit, axis=-1, keepdims=True)
    grad_field = scale * (grad_unit - mean_grad - unit * mean_cross)
    return grad_field, jnp.sum(grad * unit, axis=0), jnp.sum(grad, axis=0)


def slot_table(route_ids, mp_index):
    tokens = route_ids.shape[0]
    order = jnp.arange(lax.axis_size("x"), dtype=jnp.int32)
    named = jnp.any(route_ids.T[None, :, :] == order[:, None, None], axis=1)
    steps = jnp.arange(tokens, dtype=jnp.int32)
    earlier = (steps[:, None] < steps[None, :]).astype(BF16)
    position = dot(named.astype(BF16), earlier, ((1,), (0,))).astype(jnp.int32)
    slots = jnp.arange(CAP // 2, dtype=jnp.int32) + mp_index * (CAP // 2)
    return named[:, None, :] & (position[:, None, :] == slots[None, :, None])


def to_experts(half):
    own = all_to_all(half, "x").reshape(-1, half.shape[2])
    return jnp.concatenate([own, swap(own, "mp")], axis=0)


def from_experts(partial, experts):
    rows = partial.shape[0] // 2
    other = swap(partial[rows:].astype(BF16), "mp")
    own = (partial[:rows] + other.astype(F32)).astype(BF16)
    own = own.reshape(experts, rows // experts, -1)
    return all_to_all(own, "x").reshape(rows, -1)


def forward_layer(dense, experts_pair, tokens, table, beside):
    qkv, out_t, gain_one, shift_one, gain_two, shift_two, router = dense
    first, second = experts_pair[0], experts_pair[1]
    count, width = tokens.shape
    experts = table.shape[0]
    half_width = out_t.shape[1]
    heads = half_width // HEAD_DIM
    unit_one, scale_one = normalise(tokens)
    normed_one = (unit_one * gain_one[None, :] + shift_one[None, :]).astype(BF16)
    projected = dot(normed_one, qkv, ((1,), (0,))).astype(BF16)
    parts = projected.reshape(count, 3, heads, HEAD_DIM)
    queries, keys_all, values_all = parts[:, 0], parts[:, 1], parts[:, 2]
    scores = jnp.einsum(
        "qhe,khe->hqk", queries, keys_all, preferred_element_type=F32
    ) * HEAD_DIM ** (-0.5)
    probability = jax.nn.softmax(scores, axis=-1)
    prob_low = probability.astype(BF16)
    mixed = (
        jnp.einsum("hqk,khe->qhe", prob_low, values_all, preferred_element_type=F32)
        .astype(BF16)
        .reshape(count, half_width)
    )
    attended = dot(mixed, out_t, ((1,), (1,)))
    attended = attended + swap(attended, "mp")
    hidden = tokens + attended
    unit_two, scale_two = normalise(hidden)
    normed_two = (unit_two * gain_two[None, :] + shift_two[None, :]).astype(BF16)
    gates = jax.nn.softmax(dot(router, normed_two, ((0,), (1,))), axis=0)
    select = table.astype(BF16).reshape(-1, count)
    slot_gates = jnp.sum(jnp.where(table, gates[:, None, :], 0.0), axis=2).reshape(-1, 1)
    dispatched = to_experts(
        dot(select, normed_two, ((1,), (0,))).astype(BF16).reshape(experts, -1, width)
    )
    if beside is not None:
        dispatched, beside = lax.optimization_barrier((dispatched, beside))
    inner_pre = dot(dispatched, first, ((1,), (0,)))
    below = 0.5 * (1.0 + lax.erf(inner_pre * 0.5**0.5))
    activated = (inner_pre * below).astype(BF16)
    expert_sum = from_experts(dot(activated, second, ((1,), (1,))), experts)
    weighted = (slot_gates * expert_sum.astype(F32)).astype(BF16)
    mixture = dot(select, weighted, ((0,), (0,)))
    output = hidden + (mixture + swap(mixture, "mp"))
    saved = (
        unit_one,
        scale_one,
        normed_one,
        queries,
        keys_all,
        values_all,
        probability,
        prob_low,
        mixed,
        unit_two,
        scale_two,
        normed_two,
        gates,
        table,
        select,
        slot_gates,
        dispatched,
        inner_pre,
        below,
        activated,
        expert_sum,
    )
    return output.astype(BF16), saved, beside


def together(value, others):
    joined = lax.optimization_barrier((value,) + tuple(others))
    return joined[0], joined[1:]


def backward_layer(dense, experts_pair, saved, grad_low, pack, early, late):
    qkv, out_t, gain_one, shift_one, gain_two, shift_two, router = dense
    first, second = experts_pair[0], experts_pair[1]
    (
        unit_one,
        scale_one,
        normed_one,
        queries,
        keys_all,
        values_all,
        probability,
        prob_low,
        mixed,
        unit_two,
        scale_two,
        normed_two,
        gates,
        table,
        select,
        slot_gates,
        dispatched,
        inner_pre,
        below,
        activated,
        expert_sum,
    ) = saved
    experts = table.shape[0]
    count, width = grad_low.shape
    grad_output = grad_low.astype(F32)
    grad_slots = dot(select, grad_low, ((1,), (0,)))
    slot_chosen = jnp.sum(grad_slots * expert_sum.astype(F32), axis=1).reshape(experts, -1, 1)
    grad_gates = jnp.sum(jnp.where(table, slot_chosen, 0.0), axis=1)
    grad_gates = grad_gates + swap(grad_gates, "mp")
    grad_expert = to_experts(
        (slot_gates * grad_slots).astype(BF16).reshape(experts, -1, width)
    )
    if pack is not None:
        grad_expert, (pack,) = together(grad_expert, (pack,))
        pack = all_to_all(pack, "x")
    grad_act = dot(grad_expert, second, ((1,), (0,)))
    density = jnp.exp(-0.5 * inner_pre * inner_pre) * (2.0 * 3.141592653589793) ** -0.5
    grad_inner = (grad_act * (below + inner_pre * density)).astype(BF16)
    grad_second = dot(grad_expert, activated, ((0,), (0,))).astype(BF16)
    grad_first = dot(dispatched, grad_inner, ((0,), (0,))).astype(BF16)
    grad_rows = dot(grad_inner, first, ((1,), (1,)))
    if pack is not None:
        grad_rows, (pack,) = together(grad_rows, (pack,))
    grad_dispatched = from_experts(grad_rows, experts)
    pair = jnp.stack([grad_first, grad_second])
    grad_dispatched, (pair, *early) = together(grad_dispatched, (pair,) + early)
    expert_grads = lax.psum_scatter(pair, "g", scatter_dimension=1, tiled=True)
    returned = dot(select, grad_dispatched, ((0,), (0,)))
    returned = returned + swap(returned, "mp")
    grad_logits = gates * (grad_gates - jnp.sum(gates * grad_gates, axis=0, keepdims=True))
    grad_router = dot(normed_two.astype(F32), grad_logits, ((0,), (1,)), PRECISE)
    grad_normed = returned + dot(grad_logits, router.astype(F32), ((0,), (1,)), PRECISE)
    grad_hidden, grad_gain_two, grad_shift_two = norm_back(
        grad_normed, unit_two, scale_two, gain_two
    )
    grad_hidden = grad_output + grad_hidden
    grad_attended = grad_hidden.astype(BF16)
    grad_out_t = dot(grad_attended, mixed, ((0,), (0,)))
    grad_mixed = dot(grad_attended, out_t, ((1,), (0,))).astype(BF16).reshape(queries.shape)
    grad_prob = jnp.einsum("qhe,khe->hqk", grad_mixed, values_all, preferred_element_type=F32)
    grad_values = jnp.einsum("hqk,qhe->khe", prob_low, grad_mixed, preferred_element_type=F32)
    grad_scores = (
        probability * (grad_prob - jnp.sum(probability * grad_prob, axis=-1, keepdims=True))
    ).astype(BF16)
    grad_queries = jnp.einsum(
        "hqk,khe->qhe", grad_scores, keys_all, preferred_element_type=F32
    ) * HEAD_DIM ** (-0.5)
    grad_keys = jnp.einsum(
        "hqk,qhe->khe", grad_scores, queries, preferred_element_type=F32
    ) * HEAD_DIM ** (-0.5)
    grad_projected = (
        jnp.stack([grad_queries, grad_keys, grad_values], axis=1).astype(BF16).reshape(count, -1)
    )
    if late:
        grad_projected, late = together(grad_projected, late)
    grad_qkv = dot(normed_one, grad_projected, ((0,), (0,)))
    grad_normed = dot(grad_projected, qkv, ((1,), (1,)))
    grad_normed = grad_normed + swap(grad_normed, "mp")
    grad_tokens, grad_gain_one, grad_shift_one = norm_back(
        grad_normed, unit_one, scale_one, gain_one
    )
    vectors = jnp.stack([grad_gain_one, grad_shift_one, grad_gain_two, grad_shift_two], axis=1)
    dense_grads = (grad_qkv, grad_out_t, vectors, grad_router)
    grad_low = (grad_hidden + grad_tokens).astype(BF16)
    return grad_low, dense_grads, expert_grads, pack, early, late


def shards(
    inputs,
    cotangent,
    routes,
    gain_one,
    shift_one,
    qkv_weight,
    out_weight,
    gain_two,
    shift_two,
    router,
    expert_in,
    expert_out,
):
    section = lax.axis_index("section")
    mp_index = lax.axis_index("mp")
    size_g = lax.axis_size("g")
    size_x = lax.axis_size("x")
    rows = qkv_weight.shape[1]
    width = rows * size_g * size_x
    half_width = out_weight.shape[1]
    first_section = section == 0

    def by_layer(own):
        other = swap(own, "section")
        return jnp.where(first_section, own, other), jnp.where(first_section, other, own)

    small = jnp.stack([gain_one[0], shift_one[0], gain_two[0], shift_two[0]], axis=1)
    dense_shard = jnp.concatenate(
        [
            qkv_weight[0].reshape(rows, 3 * half_width),
            out_weight[0].T,
            small,
            router[0],
            jnp.zeros((rows, 120), BF16),
        ],
        axis=1,
    )
    expert_shard = jnp.stack([expert_in[0], jnp.swapaxes(expert_out[0], 1, 2)], axis=1)
    routes_own = routes[0, :, 0]
    routes_kept = piece(routes_own, section)
    routes_other = swap(piece(routes_own, 1 - section), "section")
    routes_pair = (
        jnp.where(first_section, routes_kept, routes_other),
        jnp.where(first_section, routes_other, routes_kept),
    )

    full = 3 * half_width

    expert_own = all_to_all(expert_shard, "x")
    expert_own = jnp.swapaxes(expert_own, 0, 1).reshape(2, size_x * rows, -1)
    both = jnp.stack(by_layer(dense_shard))
    both = all_to_all(jnp.broadcast_to(both[None], (size_g,) + both.shape), "g")

    def gathered(layer):
        block = both[:, layer]
        block = all_to_all(jnp.broadcast_to(block[None], (size_x,) + block.shape), "x")
        return jnp.swapaxes(block, 0, 1).reshape(width, -1)

    def dense_weights(pack):
        extra = pack[:, full + half_width : full + half_width + 8]
        vectors = extra[:, :4].astype(F32).T
        return (
            pack[:, :full],
            pack[:, full : full + half_width],
            vectors[0],
            vectors[1],
            vectors[2],
            vectors[3],
            extra[:, 4:],
        )

    expert_all = lax.all_gather(expert_own, ("section", "g"), axis=0, tiled=False)
    expert_all = expert_all.reshape(2, size_g, 2, size_x * rows, -1)
    experts_here = tuple(
        (
            tuple((expert_all[layer, :, i].reshape(width, -1) for i in range(2)))
            for layer in range(2)
        )
    )
    pack_zero = gathered(0)
    pack_one = gathered(1)
    dense_zero = dense_weights(pack_zero)
    tables = tuple((slot_table(r, mp_index) for r in routes_pair))
    tokens = piece(inputs[:, 0], section)
    out_zero, saved_zero, pack_one = forward_layer(
        dense_zero, experts_here[0], tokens.astype(F32), tables[0], pack_one
    )
    dense_one = dense_weights(pack_one)
    out_one, saved_one, unused = forward_layer(
        dense_one, experts_here[1], out_zero.astype(F32), tables[1], None
    )

    def by_section(zero, one):
        own = jnp.where(first_section, zero, one)
        other = swap(jnp.where(first_section, one, zero), "section")
        low = jnp.where(first_section, own, other)
        high = jnp.where(first_section, other, own)
        return jnp.stack([low, high])[None, :, None]

    def section_sum(zero, one):
        own = jnp.where(first_section, zero, one)
        other = swap(jnp.where(first_section, one, zero), "section")
        return own.astype(F32) + other.astype(F32)

    acts = by_section(out_zero, out_one)

    def owned_experts(own):
        own = own.astype(BF16).reshape(2, size_x, rows, -1)
        return all_to_all(jnp.swapaxes(own, 0, 1), "x")

    def packed(grads):
        pack = jnp.concatenate(list(grads) + [jnp.zeros((width, 120), F32)], axis=1)
        return jnp.swapaxes(pack.astype(BF16).reshape(size_g, size_x, rows, -1), 0, 1)

    grad_mid, grads_one, expert_one, unused, (acts,), unused = backward_layer(
        dense_one, experts_here[1], saved_one, piece(cotangent[:, 0], section), None, (acts,), ()
    )
    grad_in, grads_zero, expert_zero, pack_one, unused, late = backward_layer(
        dense_zero,
        experts_here[0],
        saved_zero,
        grad_mid,
        packed(grads_one),
        (),
        (owned_experts(expert_one),),
    )
    pack_zero = all_to_all(packed(grads_zero), "x")
    dense_both = jnp.stack([summed(pack_zero), summed(pack_one)], axis=1).astype(BF16)
    dense_both = summed(all_to_all(dense_both, "g"))
    dense_sum = section_sum(dense_both[0], dense_both[1])
    expert_sum = section_sum(owned_experts(expert_zero), late[0])
    input_grads = by_section(grad_in, grad_mid)
    grad_first = expert_sum[:, 0]
    grad_second = jnp.swapaxes(expert_sum[:, 1], 1, 2)
    grad_qkv = dense_sum[:, :full].reshape(rows, 3, half_width)
    grad_out = dense_sum[:, full : full + half_width].T
    tail = dense_sum[:, full + half_width :]
    outs = (
        tail[:, 0],
        tail[:, 1],
        grad_qkv,
        grad_out,
        tail[:, 2],
        tail[:, 3],
        tail[:, 4:8],
        grad_first,
        grad_second,
    )
    return (acts, input_grads) + tuple((member[None] for member in outs))


def solution(mesh):
    sections, batch, pair = mesh.devices.shape
    inner = Mesh(mesh.devices.reshape(sections, batch // 4, 4, pair), ("section", "g", "x", "mp"))
    dp = ("g", "x")
    placed = (
        P(None, dp, None, None),
        P(None, dp, None, None),
        P("section", None, dp, None, None),
        P("section", dp),
        P("section", dp),
        P("section", dp, None, "mp"),
        P("section", "mp", dp),
        P("section", dp),
        P("section", dp),
        P("section", dp, None),
        P("section", None, dp, "mp"),
        P("section", None, "mp", dp),
    )
    return jax.shard_map(
        shards,
        mesh=inner,
        in_specs=placed,
        out_specs=(
            P("section", None, dp, None, None),
            P("section", None, dp, None, None),
            P("section", dp),
            P("section", dp),
            P("section", dp, None, "mp"),
            P("section", "mp", dp),
            P("section", dp),
            P("section", dp),
            P("section", dp, None),
            P("section", None, dp, "mp"),
            P("section", None, "mp", dp),
        ),
        check_vma=False,
    )
```

time: 784 us -> 561 us (0.72)
  starting transfers between devices: 345 us -> 58.3 us
  blocking collectives: 0 us -> 86.7 us
  local copies, waits for them, and re-layouts: 95.9 us -> 68.1 us
  waiting for transfers between devices: 217 us -> 200 us
  between operations: 4.56 us -> 16.1 us
  other arithmetic: 34.1 us -> 44.8 us
    ppermute x194 -> x24, starting transfers between devices: 326 us -> 11 us  [swap(): return lax.ppermute(block, axis, [(i, i ^ distance) for i in range(size)])]
    ppermute x194 -> x24, waiting for transfers between devices: 210 us -> 39.9 us  [swap(): return lax.ppermute(block, axis, [(i, i ^ distance) for i in range(size)])]
    all_to_all x0 -> x12, waiting for transfers between devices: none -> 160 us  [all_to_all(): return lax.all_to_all(blocks, axis, 0, 0, tiled=True)]
    all_to_all x0 -> x5, blocking collectives: none -> 86.7 us  [all_to_all(): return lax.all_to_all(blocks, axis, 0, 0, tiled=True)]
    all_to_all x0 -> x12, starting transfers between devices: none -> 47.2 us  [all_to_all(): return lax.all_to_all(blocks, axis, 0, 0, tiled=True)]
    dynamic_update_slice x83 -> x0, local copies, waits for them, and re-layouts: 27.2 us -> none  [the longest x75 27.1 us: gathered(): lax.dynamic_update_slice_in_dim(total, jnp.expand_dims(arrived, place), o...]
    ppermute x8 -> x0, starting transfers between devices: 18.9 us -> none  [send_one_way(): return lax.ppermute(block, axis, [(source, target)])]
    another operation x6 -> x5, other arithmetic: 0.31 us -> 8.76 us  [the longest x2 7.52 us: backward_layer(): pair = jnp.stack([grad_first, grad_second])]
  transfers between devices with their start and end apart: 202 -> 39, of which waited for: 67 -> 23; matrix products, arithmetic and copies ran while one was open for 20% -> 28% of each run, Pallas kernels for 0% -> 0%
where the time goes in v2:
time: 561 us; the launch traced here: 551 us
  waiting for transfers between devices  200 us (36%)
  blocking collectives  86.7 us (15%)
  matrix products  77.3 us (14%)
  local copies, waits for them, and re-layouts  68.1 us (12%)
  starting transfers between devices  58.3 us (10%)
  other arithmetic  44.8 us (8%)
  between operations  16.1 us (3%)
    all_to_all x12, waiting for transfers between devices, all_to_all(): return lax.all_to_all(blocks, axis, 0, 0, tiled=True)  160 us
    all_to_all x5, blocking collectives, all_to_all(): return lax.all_to_all(blocks, axis, 0, 0, tiled=True)  86.7 us
    dot_general x40, matrix products, dot(): lax.dot_general(a, b, (dims, ((), ())), precision=precision, preferred_el...  66.1 us
    all_to_all x12, starting transfers between devices, all_to_all(): return lax.all_to_all(blocks, axis, 0, 0, tiled=True)  47.2 us
    ppermute x24, waiting for transfers between devices, swap(): return lax.ppermute(block, axis, [(i, i ^ distance) for i in range(size)])  39.9 us
    concatenate x11, local copies, waits for them, and re-layouts, packed(): pack = jnp.concatenate(list(grads) + [jnp.zeros((width, 120), F32)], axis=1)  18.3 us
    unnamed x221, local copies, waits for them, and re-layouts  11.4 us
  transfers between devices with their start and end apart: 39, of which 23 were waited for; matrix products, arithmetic and copies ran while one was open for 28% of the time, Pallas kernels for 0%

profile of v2, /device:TPU:16, one launch (start us, length us, event | category | flops | bytes accessed | tf_op | source)
XLA Modules:
  0.0 551.0 jit_solution(940342215716009782)
XLA Ops:
  8.5 14.3 %all_to_all.85 = bf16[4,2,24,1536]{3,2,1,0:T(8,128)(2,1)S(1)} all-to-all(bf16[4,2,24,1536]{3,2,1,0:T(8,128)(2,1)S(1)} %pad_maximum_fusion.7), channel_id=1, replica_groups=mesh['section'=2,'g'=8,'x'=4,'mp'=2] {'x'}, dimensions={0} | all-to-all | bytes 1179648 | tf_op jit(solution)/shard_map/all_to_all | solution.py:30
  29.0 38.2 %all_to_all.86 = bf16[8,2,24,1664]{3,2,1,0:T(8,128)(2,1)S(1)} all-to-all(bf16[8,2,24,1664]{3,2,1,0:T(8,128)(2,1)S(1)} %broadcast_in_dim.61), channel_id=1, replica_groups=mesh['section'=2,'g'=8,'x'=4,'mp'=2] {'g'}, dimensions={0} | all-to-all | bytes 2555904 | tf_op jit(solution)/shard_map/all_to_all | solution.py:30
  69.7 3.8 all-to-all-start.1
  77.2 25.4 %all-to-all-done.1 = bf16[4,8,24,1664]{3,2,1,0:T(8,128)(2,1)S(1)} async-done(((bf16[4,8,24,1664]{3,2,1,0:T(8,128)(2,1)}), bf16[4,8,24,1664]{3,2,1,0:T(8,128)(2,1)S(1)}, u32[]{:S(2)}, u32[]{:S(2)}) %all-to-all-start.1) | async-done | bytes 2555936 | tf_op jit(solution)/shard_map/all_to_all | solution.py:30
  111.6 11.7 %all_to_all.87 = bf16[4,64,768]{2,1,0:T(8,128)(2,1)} all-to-all(bf16[4,64,768]{2,1,0:T(8,128)(2,1)S(1)} %bitcast.408), channel_id=1, replica_groups=mesh['section'=2,'g'=8,'x'=4,'mp'=2] {'x'}, dimensions={0} | all-to-all | bytes 786432 | tf_op jit(solution)/shard_map/all_to_all | solution.py:30
  125.1 3.7 all-to-all-start.3
  128.8 30.9 %all-to-all-done.3 = bf16[4,8,24,1664]{3,2,1,0:T(8,128)(2,1)S(1)} async-done(((bf16[4,8,24,1664]{3,2,1,0:T(8,128)(2,1)}), bf16[4,8,24,1664]{3,2,1,0:T(8,128)(2,1)S(1)}, u32[]{:S(2)}, u32[]{:S(2)}) %all-to-all-start.3) | async-done | bytes 2555936 | tf_op jit(solution)/shard_map/all_to_all | solution.py:30
  162.5 5.9 %fusion.132 = (bf16[1,8,1,96,1536]{4,3,2,1,0:T(8,128)(2,1)}, bf16[1,8,1,96,1536]{4,3,2,1,0:T(8,128)(2,1)}, bf16[1,8,1,96,1536]{4,3,2,1,0:T(8,128)(2,1)S(1)}, bf16[1,8,1,96,1536]{4,3,2,1,0:T(8,128)(2,1)S(1)}) fusion(bf16[2,8,2,96,1536]{4,3,2,1,0:T(8,128)(2,1)} %bitcast.366), kind=kLoop, calls=%fused_computation.304 | loop fusion | bytes 18874368 | tf_op jit(solution)/shard_map/slice | solution.py:315
  179.4 8.4 %all-to-all-done.5 = bf16[4,64,768]{2,1,0:T(8,128)(2,1)S(1)} async-done(((bf16[4,64,768]{2,1,0:T(8,128)(2,1)}), bf16[4,64,768]{2,1,0:T(8,128)(2,1)S(1)}, u32[]{:S(2)}, u32[]{:S(2)}) %all-to-all-start.5) | async-done | bytes 393248 | tf_op jit(solution)/shard_map/all_to_all | solution.py:30
  198.5 11.2 %all_to_all.88 = bf16[4,64,768]{2,1,0:T(8,128)(2,1)S(1)} all-to-all(bf16[4,64,768]{2,1,0:T(8,128)(2,1)S(1)} %bitcast.409), channel_id=1, replica_groups=mesh['section'=2,'g'=8,'x'=4,'mp'=2] {'x'}, dimensions={0} | all-to-all | bytes 786432 | tf_op jit(solution)/shard_map/all_to_all | solution.py:30
  222.3 8.6 %all-to-all-done.9 = bf16[4,64,768]{2,1,0:T(8,128)(2,1)S(1)} async-done(((bf16[4,64,768]{2,1,0:T(8,128)(2,1)}), bf16[4,64,768]{2,1,0:T(8,128)(2,1)S(1)}, u32[]{:S(2)}, u32[]{:S(2)}) %all-to-all-start.9) | async-done | bytes 393248 | tf_op jit(solution)/shard_map/all_to_all | solution.py:30
  234.9 11.3 %all_to_all.89 = bf16[4,64,768]{2,1,0:T(8,128)(2,1)S(1)} all-to-all(bf16[4,64,768]{2,1,0:T(8,128)(2,1)S(1)} %bitcast.415), channel_id=1, replica_groups=mesh['section'=2,'g'=8,'x'=4,'mp'=2] {'x'}, dimensions={0} | all-to-all | bytes 786432 | tf_op jit(solution)/shard_map/all_to_all | solution.py:30
  267.8 6.8 %all-to-all-done.8 = bf16[4,64,768]{2,1,0:T(8,128)(2,1)S(1)} async-done(((bf16[4,64,768]{2,1,0:T(8,128)(2,1)}), bf16[4,64,768]{2,1,0:T(8,128)(2,1)S(1)}, u32[]{:S(2)}, u32[]{:S(2)}) %all-to-all-start.8) | async-done | bytes 393248 | tf_op jit(solution)/shard_map/all_to_all | solution.py:30
  297.9 4.2 all-to-all-start.10
  304.4 6.5 %all-to-all-done.10 = bf16[4,64,768]{2,1,0:T(8,128)(2,1)} async-done(((bf16[4,64,768]{2,1,0:T(8,128)(2,1)}), bf16[4,64,768]{2,1,0:T(8,128)(2,1)}, u32[]{:S(2)}, u32[]{:S(2)}) %all-to-all-start.10) | async-done | bytes 393248 | tf_op jit(solution)/shard_map/all_to_all | solution.py:30
  319.1 4.0 concatenate.58
  326.9 3.9 all-to-all-start.11
  330.8 4.9 fusion.15
  339.5 23.4 %all-to-all-done.11 = bf16[4,8,24,1664]{3,2,1,0:T(8,128)(2,1)S(1)} async-done(((bf16[4,8,24,1664]{3,2,1,0:T(8,128)(2,1)}), bf16[4,8,24,1664]{3,2,1,0:T(8,128)(2,1)S(1)}, u32[]{:S(2)}, u32[]{:S(2)}) %all-to-all-start.11) | async-done | bytes 2555936 | tf_op jit(solution)/shard_map/all_to_all | solution.py:30
  364.2 4.7 fusion.13
  372.5 4.1 all-to-all-start.12
  376.7 5.0 pad_maximum_fusion.1
  381.7 3.9 all-to-all-done.12
  403.3 4.2 all-to-all-start.13
  411.5 6.9 %all-to-all-done.13 = bf16[4,2,24,1536]{3,2,1,0:T(8,128)(2,1)} async-done(((bf16[4,2,24,1536]{3,2,1,0:T(8,128)(2,1)}), bf16[4,2,24,1536]{3,2,1,0:T(8,128)(2,1)}, u32[]{:S(2)}, u32[]{:S(2)}) %all-to-all-start.13) | async-done | bytes 589856 | tf_op jit(solution)/shard_map/all_to_all | solution.py:30
  437.2 5.4 concatenate.64
  445.9 4.5 all-to-all-start.14
  451.8 30.9 %all-to-all-done.14 = bf16[4,8,24,1664]{3,2,1,0:T(8,128)(2,1)} async-done(((bf16[4,8,24,1664]{3,2,1,0:T(8,128)(2,1)}), bf16[4,8,24,1664]{3,2,1,0:T(8,128)(2,1)}, u32[]{:S(2)}, u32[]{:S(2)}) %all-to-all-start.14) | async-done | bytes 2555936 | tf_op jit(solution)/shard_map/all_to_all | solution.py:30
  486.1 4.9 all-to-all-start.15
  494.8 18.0 %collective-permute-done.21 = bf16[197,768]{1,0:T(8,128)(2,1)S(1)} collective-permute-done((bf16[197,768]{1,0:T(8,128)(2,1)S(1)}, bf16[197,768]{1,0:T(8,128)(2,1)S(1)}, u32[]{:S(2)}, u32[]{:S(2)}) %collective-permute-start.21) | collective-permute-done | bytes 302624 | tf_op jit(solution)/shard_map/ppermute | solution.py:22
  520.7 8.2 %all-to-all-done.16 = bf16[4,2,24,1536]{3,2,1,0:T(8,128)(2,1)S(1)} async-done(((bf16[4,2,24,1536]{3,2,1,0:T(8,128)(2,1)}), bf16[4,2,24,1536]{3,2,1,0:T(8,128)(2,1)S(1)}, u32[]{:S(2)}, u32[]{:S(2)}) %all-to-all-start.16) | async-done | bytes 589856 | tf_op jit(solution)/shard_map/all_to_all | solution.py:30
  533.0 9.7 %collective-permute-done.23 = bf16[4,2,24,1536]{3,2,1,0:T(8,128)(2,1)S(1)} collective-permute-done((bf16[4,2,24,1536]{3,2,1,0:T(8,128)(2,1)S(1)}, bf16[4,2,24,1536]{3,2,1,0:T(8,128)(2,1)S(1)}, u32[]{:S(2)}, u32[]{:S(2)}) %collective-permute-start.23) | collective-permute-done | bytes 589856 | tf_op jit(solution)/shard_map/ppermute | solution.py:22
  (466 shorter events, 197.6 us)
Async XLA Ops:
  7.3 155.2 %all-gather.2.cloned.1.call-start = ((), (), s32[]{:S(2)}) async-start(), calls=%async_computation.19 | async-start | bytes 10027008 | tf_op jit(solution)/shard_map/all_gather | solution.py:311
  24.3 4.5 collective-permute-start.1
  69.7 32.9 %all-to-all-start.1 = ((bf16[4,8,24,1664]{3,2,1,0:T(8,128)(2,1)}), bf16[4,8,24,1664]{3,2,1,0:T(8,128)(2,1)S(1)}, u32[]{:S(2)}, u32[]{:S(2)}) async-start(bf16[4,8,24,1664]{3,2,1,0:T(8,128)(2,1)} %broadcast_in_dim.63), calls=%async_computation.1 | async-start | bytes 5111808 | tf_op jit(solution)/shard_map/all_to_all | solution.py:30
  73.6 3.7 collective-permute-start
  125.1 34.6 %all-to-all-start.3 = ((bf16[4,8,24,1664]{3,2,1,0:T(8,128)(2,1)}), bf16[4,8,24,1664]{3,2,1,0:T(8,128)(2,1)S(1)}, u32[]{:S(2)}, u32[]{:S(2)}) async-start(bf16[4,8,24,1664]{3,2,1,0:T(8,128)(2,1)} %broadcast_in_dim.65), calls=%async_computation.3 | async-start | bytes 5111808 | tf_op jit(solution)/shard_map/all_to_all | solution.py:30
  128.8 32.6 %collective-permute-start.3 = (bf16[256,768]{1,0:T(8,128)(2,1)}, bf16[256,768]{1,0:T(8,128)(2,1)}, u32[]{:S(2)}, u32[]{:S(2)}) collective-permute-start(bf16[256,768]{1,0:T(8,128)(2,1)} %bitcast.410), channel_id=1, source_target_pairs={{0,1},{1,0},{2,3},{3,2},{4,5},{5,4},{6,7},{7,6},{8,9},{9,8},{10,11... | collective-permute-start | bytes 1179656 | tf_op jit(solution)/shard_map/ppermute | solution.py:22
  175.7 12.1 %all-to-all-start.5 = ((bf16[4,64,768]{2,1,0:T(8,128)(2,1)}), bf16[4,64,768]{2,1,0:T(8,128)(2,1)S(1)}, u32[]{:S(2)}, u32[]{:S(2)}) async-start(bf16[4,64,768]{2,1,0:T(8,128)(2,1)} %bitcast.41), calls=%async_computation.5 | async-start | bytes 786432 | tf_op jit(solution)/shard_map/all_to_all | solution.py:30
  188.2 2.6 collective-permute-start.5
  218.8 12.1 %all-to-all-start.9 = ((bf16[4,64,768]{2,1,0:T(8,128)(2,1)}), bf16[4,64,768]{2,1,0:T(8,128)(2,1)S(1)}, u32[]{:S(2)}, u32[]{:S(2)}) async-start(bf16[4,64,768]{2,1,0:T(8,128)(2,1)} %bitcast.414), calls=%async_computation.9 | async-start | bytes 786432 | tf_op jit(solution)/shard_map/all_to_all | solution.py:30
  233.4 12.9 %collective-permute-start.11 = (f32[197,768]{1,0:T(8,128)S(1)}, f32[197,768]{1,0:T(8,128)S(1)}, u32[]{:S(2)}, u32[]{:S(2)}) collective-permute-start(f32[197,768]{1,0:T(8,128)S(1)} %convolution_bitcast_fusion), channel_id=1, source_target_pairs={{0,1},{1,0},{2,3},{3,2},{4,5},{5,4},{6,7},{7,6},{8,9},{9,8},{10,11... | collective-permute-start | bytes 1815560 | tf_op jit(solution)/shard_map/ppermute | solution.py:22
  246.3 3.6 collective-permute-start.7
  247.3 18.5 %collective-permute-start.12 = (bf16[197,768]{1,0:T(8,128)(2,1)}, bf16[197,768]{1,0:T(8,128)(2,1)}, u32[]{:S(2)}, u32[]{:S(2)}) collective-permute-start(bf16[197,768]{1,0:T(8,128)(2,1)} %get-tuple-element.134), channel_id=1, source_target_pairs={{0,64},{64,0},{1,65},{65,1},{2,66},{66,2},{3,67},{67,3},{4,68},{68... | collective-permute-start | bytes 907784 | tf_op jit(solution)/shard_map/ppermute | solution.py:22
  254.5 5.8 %collective-permute-start.9 = (bf16[256,768]{1,0:T(8,128)(2,1)}, bf16[256,768]{1,0:T(8,128)(2,1)}, u32[]{:S(2)}, u32[]{:S(2)}) collective-permute-start(bf16[256,768]{1,0:T(8,128)(2,1)} %slice.347), channel_id=1, source_target_pairs={{0,1},{1,0},{2,3},{3,2},{4,5},{5,4},{6,7},{7,6},{8,9},{9,8},{10,11... | collective-permute-start | bytes 1179656 | tf_op jit(solution)/shard_map/ppermute | solution.py:22
  262.3 12.2 %all-to-all-start.8 = ((bf16[4,64,768]{2,1,0:T(8,128)(2,1)}), bf16[4,64,768]{2,1,0:T(8,128)(2,1)S(1)}, u32[]{:S(2)}, u32[]{:S(2)}) async-start(bf16[4,64,768]{2,1,0:T(8,128)(2,1)} %bitcast.412), calls=%async_computation.8 | async-start | bytes 786432 | tf_op jit(solution)/shard_map/all_to_all | solution.py:30
  265.8 135.5 %reduce-scatter.3.cloned.1.call-start = ((), (), s32[]{:S(2)}) async-start(), calls=%async_computation.20 | async-start | bytes 5308416 | tf_op jit(solution)/shard_map/reduce_scatter | solution.py:198
  276.6 2.8 collective-permute-start.13
  290.1 2.3 collective-permute-start.15
  297.9 13.0 %all-to-all-start.10 = ((bf16[4,64,768]{2,1,0:T(8,128)(2,1)}), bf16[4,64,768]{2,1,0:T(8,128)(2,1)}, u32[]{:S(2)}, u32[]{:S(2)}) async-start(bf16[4,64,768]{2,1,0:T(8,128)(2,1)} %bitcast.78), calls=%async_computation.10 | async-start | bytes 786432 | tf_op jit(solution)/shard_map/all_to_all | solution.py:30
  310.9 12.2 %collective-permute-start.16 = (bf16[256,768]{1,0:T(8,128)(2,1)}, bf16[256,768]{1,0:T(8,128)(2,1)}, u32[]{:S(2)}, u32[]{:S(2)}) collective-permute-start(bf16[256,768]{1,0:T(8,128)(2,1)} %bitcast.79), channel_id=1, source_target_pairs={{0,1},{1,0},{2,3},{3,2},{4,5},{5,4},{6,7},{7,6},{8,9},{9,8},{10,11... | collective-permute-start | bytes 1179656 | tf_op jit(solution)/shard_map/ppermute | solution.py:22
  326.9 36.0 %all-to-all-start.11 = ((bf16[4,8,24,1664]{3,2,1,0:T(8,128)(2,1)}), bf16[4,8,24,1664]{3,2,1,0:T(8,128)(2,1)S(1)}, u32[]{:S(2)}, u32[]{:S(2)}) async-start(bf16[4,8,24,1664]{3,2,1,0:T(8,128)(2,1)} %copy.227), calls=%async_computation.11 | async-start | bytes 5111808 | tf_op jit(solution)/shard_map/all_to_all | solution.py:30
  364.1 7.6 %collective-permute-start.17 = (bf16[256,768]{1,0:T(8,128)(2,1)S(1)}, bf16[256,768]{1,0:T(8,128)(2,1)S(1)}, u32[]{:S(2)}, u32[]{:S(2)}) collective-permute-start(bf16[256,768]{1,0:T(8,128)(2,1)S(1)} %slice.345), channel_id=1, source_target_pairs={{0,1},{1,0},{2,3},{3,2},{4,5},{5,4},{6,7},{7,6},{8,9},{9,8},{10,11... | collective-permute-start | bytes 1179656 | tf_op jit(solution)/shard_map/ppermute | solution.py:22
  372.5 13.1 %all-to-all-start.12 = ((bf16[4,64,768]{2,1,0:T(8,128)(2,1)}), bf16[4,64,768]{2,1,0:T(8,128)(2,1)}, u32[]{:S(2)}, u32[]{:S(2)}) async-start(bf16[4,64,768]{2,1,0:T(8,128)(2,1)} %bitcast.413), calls=%async_computation.12 | async-start | bytes 786432 | tf_op jit(solution)/shard_map/all_to_all | solution.py:30
  376.6 137.8 %reduce-scatter.5.cloned.1.call-start = ((), (), s32[]{:S(2)}) async-start(), calls=%async_computation.21 | async-start | bytes 5308416 | tf_op jit(solution)/shard_map/reduce_scatter | solution.py:198
  387.7 3.8 collective-permute-start.18
  403.3 15.1 %all-to-all-start.13 = ((bf16[4,2,24,1536]{3,2,1,0:T(8,128)(2,1)}), bf16[4,2,24,1536]{3,2,1,0:T(8,128)(2,1)}, u32[]{:S(2)}, u32[]{:S(2)}) async-start(bf16[4,2,24,1536]{3,2,1,0:T(8,128)(2,1)} %bitcast.392), calls=%async_computation.14 | async-start | bytes 1179648 | tf_op jit(solution)/shard_map/all_to_all | solution.py:30
  421.8 5.8 %collective-permute-start.20 = (f32[197,768]{1,0:T(8,128)}, f32[197,768]{1,0:T(8,128)}, u32[]{:S(2)}, u32[]{:S(2)}) collective-permute-start(f32[197,768]{1,0:T(8,128)} %fusion.18), channel_id=1, source_target_pairs={{0,1},{1,0},{2,3},{3,2},{4,5},{5,4},{6,7},{7,6},{8,9},{9,8},{10,11... | collective-permute-start | bytes 1815560 | tf_op jit(solution)/shard_map/ppermute | solution.py:22
  445.9 36.8 %all-to-all-start.14 = ((bf16[4,8,24,1664]{3,2,1,0:T(8,128)(2,1)}), bf16[4,8,24,1664]{3,2,1,0:T(8,128)(2,1)}, u32[]{:S(2)}, u32[]{:S(2)}) async-start(bf16[4,8,24,1664]{3,2,1,0:T(8,128)(2,1)} %copy.242), calls=%async_computation.15 | async-start | bytes 5111808 | tf_op jit(solution)/shard_map/all_to_all | solution.py:30
  486.1 28.1 %all-to-all-start.15 = ((bf16[8,2,24,1664]{3,2,1,0:T(8,128)(2,1)}), bf16[8,2,24,1664]{3,2,1,0:T(8,128)(2,1)S(1)}, u32[]{:S(2)}, u32[]{:S(2)}) async-start(bf16[8,2,24,1664]{3,2,1,0:T(8,128)(2,1)} %pad_maximum_fusion.2), calls=%async_computation.16 | async-start | bytes 2555904 | tf_op jit(solution)/shard_map/all_to_all | solution.py:30
  492.5 20.3 %collective-permute-start.21 = (bf16[197,768]{1,0:T(8,128)(2,1)S(1)}, bf16[197,768]{1,0:T(8,128)(2,1)S(1)}, u32[]{:S(2)}, u32[]{:S(2)}) collective-permute-start(bf16[197,768]{1,0:T(8,128)(2,1)S(1)} %get-tuple-element.124), channel_id=1, source_target_pairs={{0,64},{64,0},{1,65},{65,1},{2,66},{66,2},{3,67},{67,3},{4,68},{68... | collective-permute-start | bytes 907784 | tf_op jit(solution)/shard_map/ppermute | solution.py:22
  516.3 12.6 %all-to-all-start.16 = ((bf16[4,2,24,1536]{3,2,1,0:T(8,128)(2,1)}), bf16[4,2,24,1536]{3,2,1,0:T(8,128)(2,1)S(1)}, u32[]{:S(2)}, u32[]{:S(2)}) async-start(bf16[4,2,24,1536]{3,2,1,0:T(8,128)(2,1)} %bitcast.362), calls=%async_computation.18 | async-start | bytes 1179648 | tf_op jit(solution)/shard_map/all_to_all | solution.py:30
  519.8 10.3 %collective-permute-start.22 = (f32[24,1664]{1,0:T(8,128)S(1)}, f32[24,1664]{1,0:T(8,128)S(1)}, u32[]{:S(2)}, u32[]{:S(2)}) collective-permute-start(f32[24,1664]{1,0:T(8,128)S(1)} %select_bitcast_fusion.4), channel_id=1, source_target_pairs={{0,64},{64,0},{1,65},{65,1},{2,66},{66,2},{3,67},{67,3},{4,68},{68... | collective-permute-start | bytes 479240 | tf_op jit(solution)/shard_map/ppermute | solution.py:22
  530.1 12.6 %collective-permute-start.23 = (bf16[4,2,24,1536]{3,2,1,0:T(8,128)(2,1)S(1)}, bf16[4,2,24,1536]{3,2,1,0:T(8,128)(2,1)S(1)}, u32[]{:S(2)}, u32[]{:S(2)}) collective-permute-start(bf16[4,2,24,1536]{3,2,1,0:T(8,128)(2,1)S(1)} %broadcast_select_fusion), channel_id=1, source_target_pairs={{0,64},{64,0},{1,65},{65,1},{2,66},{66,2},{3,67},{67,3},{4,68},{68... | collective-permute-start | bytes 1769480 | tf_op jit(solution)/shard_map/ppermute | solution.py:22
  (115 other events, 888.6 us)
Sparse Core Ops, SparseCore 0:
  23.8 122.3 all-gather.1
  275.5 81.8 reduce-scatter.2
  385.7 81.8 reduce-scatter.4

commit v3 on v2

--- a/solution.py
+++ b/solution.py
@@ -32,6 +32,19 @@
 
 def summed(blocks):
     return jnp.sum(blocks.astype(F32), axis=0)
+
+
+def xor_order(blocks, index):
+    paired = blocks.reshape((2, 2) + blocks.shape[1:])
+    paired = jnp.where((index & 1) == 1, paired[:, ::-1], paired)
+    paired = jnp.where((index & 2) == 2, paired[::-1], paired)
+    return paired.reshape(blocks.shape)
+
+
+def by_owner(grad):
+    size_g, size_x = lax.axis_size("g"), lax.axis_size("x")
+    blocks = grad.astype(BF16).reshape(size_g, size_x, -1, grad.shape[1])
+    return jnp.swapaxes(blocks, 0, 1)
 
 
 def normalise(field):
@@ -181,20 +194,19 @@
     grad_expert = to_experts(
         (slot_gates * grad_slots).astype(BF16).reshape(experts, -1, width)
     )
-    if pack is not None:
-        grad_expert, (pack,) = together(grad_expert, (pack,))
-        pack = all_to_all(pack, "x")
     grad_act = dot(grad_expert, second, ((1,), (0,)))
     density = jnp.exp(-0.5 * inner_pre * inner_pre) * (2.0 * 3.141592653589793) ** -0.5
     grad_inner = (grad_act * (below + inner_pre * density)).astype(BF16)
     grad_second = dot(grad_expert, activated, ((0,), (0,))).astype(BF16)
     grad_first = dot(dispatched, grad_inner, ((0,), (0,))).astype(BF16)
     grad_rows = dot(grad_inner, first, ((1,), (1,)))
-    if pack is not None:
-        grad_rows, (pack,) = together(grad_rows, (pack,))
     grad_dispatched = from_experts(grad_rows, experts)
     pair = jnp.stack([grad_first, grad_second])
+    if pack is not None:
+        early = early + (pack,)
     grad_dispatched, (pair, *early) = together(grad_dispatched, (pair,) + early)
+    if pack is not None:
+        pack = all_to_all(early.pop(), "x")
     expert_grads = lax.psum_scatter(pair, "g", scatter_dimension=1, tiled=True)
     returned = dot(select, grad_dispatched, ((0,), (0,)))
     returned = returned + swap(returned, "mp")
@@ -205,6 +217,7 @@
         grad_normed, unit_two, scale_two, gain_two
     )
     grad_hidden = grad_output + grad_hidden
+    blank = jnp.zeros((width, 124), BF16)
     grad_attended = grad_hidden.astype(BF16)
     grad_out_t = dot(grad_attended, mixed, ((0,), (0,)))
     grad_mixed = dot(grad_attended, out_t, ((1,), (0,))).astype(BF16).reshape(queries.shape)
@@ -222,16 +235,24 @@
     grad_projected = (
         jnp.stack([grad_queries, grad_keys, grad_values], axis=1).astype(BF16).reshape(count, -1)
     )
-    if late:
-        grad_projected, late = together(grad_projected, late)
+    if pack is not None:
+        rest = (grad_out_t, jnp.stack([grad_gain_two, grad_shift_two], axis=1), grad_router)
+        rest = jnp.concatenate([part.astype(BF16) for part in rest + (blank[:, 2:],)], axis=1)
+        rest, (pack,) = together(by_owner(rest), (pack,))
+        rest = all_to_all(rest, "x")
+        grad_projected, (rest, *late) = together(grad_projected, (rest,) + late)
     grad_qkv = dot(normed_one, grad_projected, ((0,), (0,)))
     grad_normed = dot(grad_projected, qkv, ((1,), (1,)))
     grad_normed = grad_normed + swap(grad_normed, "mp")
     grad_tokens, grad_gain_one, grad_shift_one = norm_back(
         grad_normed, unit_one, scale_one, gain_one
     )
-    vectors = jnp.stack([grad_gain_one, grad_shift_one, grad_gain_two, grad_shift_two], axis=1)
-    dense_grads = (grad_qkv, grad_out_t, vectors, grad_router)
+    ones = jnp.stack([grad_gain_one, grad_shift_one], axis=1)
+    if pack is not None:
+        dense_grads = (all_to_all(by_owner(grad_qkv), "x"), rest, ones)
+    else:
+        twos = jnp.stack([grad_gain_two, grad_shift_two], axis=1)
+        dense_grads = (grad_qkv, grad_out_t, ones, twos, grad_router, blank[:, 4:])
     grad_low = (grad_hidden + grad_tokens).astype(BF16)
     return grad_low, dense_grads, expert_grads, pack, early, late
 
@@ -308,14 +329,8 @@
             extra[:, 4:],
         )
 
-    expert_all = lax.all_gather(expert_own, ("section", "g"), axis=0, tiled=False)
-    expert_all = expert_all.reshape(2, size_g, 2, size_x * rows, -1)
-    experts_here = tuple(
-        (
-            tuple((expert_all[layer, :, i].reshape(width, -1) for i in range(2)))
-            for layer in range(2)
-        )
-    )
+    expert_all = lax.all_gather(expert_own, ("section", "g"), axis=1, tiled=True)
+    experts_here = (expert_all[:, :width], expert_all[:, width:])
     pack_zero = gathered(0)
     pack_one = gathered(1)
     dense_zero = dense_weights(pack_zero)
@@ -343,13 +358,14 @@
 
     acts = by_section(out_zero, out_one)
 
+    axis_x = lax.axis_index("x")
+
     def owned_experts(own):
-        own = own.astype(BF16).reshape(2, size_x, rows, -1)
-        return all_to_all(jnp.swapaxes(own, 0, 1), "x")
-
-    def packed(grads):
-        pack = jnp.concatenate(list(grads) + [jnp.zeros((width, 120), F32)], axis=1)
-        return jnp.swapaxes(pack.astype(BF16).reshape(size_g, size_x, rows, -1), 0, 1)
+        own = jnp.swapaxes(own.reshape(2, size_x, rows, -1), 0, 1)
+        arrived = [piece(own, axis_x)]
+        for distance in range(1, size_x):
+            arrived.append(swap(piece(own, axis_x ^ distance), "x", distance))
+        return xor_order(jnp.stack(arrived), axis_x)
 
     grad_mid, grads_one, expert_one, unused, (acts,), unused = backward_layer(
         dense_one, experts_here[1], saved_one, piece(cotangent[:, 0], section), None, (acts,), ()
@@ -359,12 +375,28 @@
         experts_here[0],
         saved_zero,
         grad_mid,
-        packed(grads_one),
+        by_owner(jnp.concatenate([part.astype(BF16) for part in grads_one], axis=1)),
         (),
         (owned_experts(expert_one),),
     )
-    pack_zero = all_to_all(packed(grads_zero), "x")
-    dense_both = jnp.stack([summed(pack_zero), summed(pack_one)], axis=1).astype(BF16)
+    qkv_zero, rest_zero, ones_zero = grads_zero
+    ones_zero = by_owner(ones_zero).reshape(size_x, -1, rows * 2)
+    total = piece(ones_zero, axis_x).astype(F32)
+    for distance in range(1, size_x):
+        arrived = swap(piece(ones_zero, axis_x ^ distance), "x", distance)
+        total = total + arrived.astype(F32)
+    ones_zero = total.reshape(size_g, rows, 2)
+    qkv_zero, rest_zero = summed(qkv_zero), summed(rest_zero)
+    dense_zero_sum = jnp.concatenate(
+        [
+            qkv_zero,
+            rest_zero[:, :, :half_width],
+            ones_zero,
+            rest_zero[:, :, half_width:-2],
+        ],
+        axis=2,
+    )
+    dense_both = jnp.stack([dense_zero_sum, summed(pack_one)], axis=1).astype(BF16)
     dense_both = summed(all_to_all(dense_both, "g"))
     dense_sum = section_sum(dense_both[0], dense_both[1])
     expert_sum = section_sum(owned_experts(expert_zero), late[0])

time: 561 us -> 525 us (0.936)
  waiting for transfers between devices: 200 us -> 162 us
  local copies, waits for them, and re-layouts: 68.1 us -> 57.4 us
  starting transfers between devices: 58.3 us -> 68.7 us
    all_to_all x12 -> x11, waiting for transfers between devices: 160 us -> 102 us  [all_to_all(): return lax.all_to_all(blocks, axis, 0, 0, tiled=True)]
    ppermute x24 -> x33, waiting for transfers between devices: 39.9 us -> 60.4 us  [swap(): return lax.ppermute(block, axis, [(i, i ^ distance) for i in range(size)])]
    ppermute x24 -> x33, starting transfers between devices: 11 us -> 25.1 us  [swap(): return lax.ppermute(block, axis, [(i, i ^ distance) for i in range(size)])]
    concatenate x11 -> x4, local copies, waits for them, and re-layouts: 18.3 us -> 13.3 us  [the longest x2 8.22 us: backward_layer(): jnp.concatenate([part.astype(BF16) for part in rest + (blank[:, 2:],)], a...]
    all_to_all x12 -> x11, starting transfers between devices: 47.2 us -> 43.5 us  [all_to_all(): return lax.all_to_all(blocks, axis, 0, 0, tiled=True)]
    unnamed x221 -> x215, local copies, waits for them, and re-layouts: 11.4 us -> 13.7 us
  transfers between devices with their start and end apart: 39 -> 47, of which waited for: 23 -> 26; matrix products, arithmetic and copies ran while one was open for 28% -> 27% of each run, Pallas kernels for 0% -> 0%
where the time goes in v3:
time: 525 us; the launch traced here: 515 us
  waiting for transfers between devices  162 us (31%)
  blocking collectives  87.2 us (17%)
  matrix products  82.5 us (16%)
  starting transfers between devices  68.7 us (13%)
  local copies, waits for them, and re-layouts  57.4 us (11%)
  other arithmetic  40.3 us (8%)
  between operations  16.1 us (3%)
    all_to_all x11, waiting for transfers between devices, all_to_all(): return lax.all_to_all(blocks, axis, 0, 0, tiled=True)  102 us
    all_to_all x5, blocking collectives, all_to_all(): return lax.all_to_all(blocks, axis, 0, 0, tiled=True)  87.2 us
    dot_general x40, matrix products, dot(): lax.dot_general(a, b, (dims, ((), ())), precision=precision, preferred_el...  71.1 us
    ppermute x33, waiting for transfers between devices, swap(): return lax.ppermute(block, axis, [(i, i ^ distance) for i in range(size)])  60.4 us
    all_to_all x11, starting transfers between devices, all_to_all(): return lax.all_to_all(blocks, axis, 0, 0, tiled=True)  43.5 us
    ppermute x33, starting transfers between devices, swap(): return lax.ppermute(block, axis, [(i, i ^ distance) for i in range(size)])  25.1 us
    unnamed x215, local copies, waits for them, and re-layouts  13.7 us
  transfers between devices with their start and end apart: 47, of which 26 were waited for; matrix products, arithmetic and copies ran while one was open for 27% of the time, Pallas kernels for 0%

profile of v3, /device:TPU:16, one launch (start us, length us, event | category | flops | bytes accessed | tf_op | source)
XLA Modules:
  0.0 514.8 jit_solution(16158850376676954881)
XLA Ops:
  8.5 14.4 %all_to_all.80 = bf16[4,2,24,1536]{3,2,1,0:T(8,128)(2,1)S(1)} all-to-all(bf16[4,2,24,1536]{3,2,1,0:T(8,128)(2,1)S(1)} %pad_maximum_fusion.7), channel_id=1, replica_groups=mesh['section'=2,'g'=8,'x'=4,'mp'=2] {'x'}, dimensions={0} | all-to-all | bytes 1179648 | tf_op jit(solution)/shard_map/all_to_all | solution.py:30
  29.1 38.1 %all_to_all.81 = bf16[8,2,24,1664]{3,2,1,0:T(8,128)(2,1)S(1)} all-to-all(bf16[8,2,24,1664]{3,2,1,0:T(8,128)(2,1)S(1)} %broadcast_in_dim.61), channel_id=1, replica_groups=mesh['section'=2,'g'=8,'x'=4,'mp'=2] {'g'}, dimensions={0} | all-to-all | bytes 2555904 | tf_op jit(solution)/shard_map/all_to_all | solution.py:30
  69.8 3.8 all-to-all-start.1
  77.4 25.5 %all-to-all-done.1 = bf16[4,8,24,1664]{3,2,1,0:T(8,128)(2,1)S(1)} async-done(((bf16[4,8,24,1664]{3,2,1,0:T(8,128)(2,1)}), bf16[4,8,24,1664]{3,2,1,0:T(8,128)(2,1)S(1)}, u32[]{:S(2)}, u32[]{:S(2)}) %all-to-all-start.1) | async-done | bytes 2555936 | tf_op jit(solution)/shard_map/all_to_all | solution.py:30
  112.8 11.7 %all_to_all.82 = bf16[4,64,768]{2,1,0:T(8,128)(2,1)} all-to-all(bf16[4,64,768]{2,1,0:T(8,128)(2,1)S(1)} %bitcast.432), channel_id=1, replica_groups=mesh['section'=2,'g'=8,'x'=4,'mp'=2] {'x'}, dimensions={0} | all-to-all | bytes 786432 | tf_op jit(solution)/shard_map/all_to_all | solution.py:30
  129.9 30.9 %all-to-all-done.3 = bf16[4,8,24,1664]{3,2,1,0:T(8,128)(2,1)S(1)} async-done(((bf16[4,8,24,1664]{3,2,1,0:T(8,128)(2,1)}), bf16[4,8,24,1664]{3,2,1,0:T(8,128)(2,1)S(1)}, u32[]{:S(2)}, u32[]{:S(2)}) %all-to-all-start.3) | async-done | bytes 2555936 | tf_op jit(solution)/shard_map/all_to_all | solution.py:30
  163.6 5.0 multiply_convert_fusion.1
  168.6 3.7 fusion.18
  178.7 8.3 %all-to-all-done.5 = bf16[4,64,768]{2,1,0:T(8,128)(2,1)S(1)} async-done(((bf16[4,64,768]{2,1,0:T(8,128)(2,1)}), bf16[4,64,768]{2,1,0:T(8,128)(2,1)S(1)}, u32[]{:S(2)}, u32[]{:S(2)}) %all-to-all-start.5) | async-done | bytes 393248 | tf_op jit(solution)/shard_map/all_to_all | solution.py:30
  198.0 11.3 %all_to_all.83 = bf16[4,64,768]{2,1,0:T(8,128)(2,1)S(1)} all-to-all(bf16[4,64,768]{2,1,0:T(8,128)(2,1)S(1)} %bitcast.433), channel_id=1, replica_groups=mesh['section'=2,'g'=8,'x'=4,'mp'=2] {'x'}, dimensions={0} | all-to-all | bytes 786432 | tf_op jit(solution)/shard_map/all_to_all | solution.py:30
  211.0 4.9 multiply_convert_fusion
  215.9 3.7 fusion.19
  225.8 8.6 %all-to-all-done.9 = bf16[4,64,768]{2,1,0:T(8,128)(2,1)S(1)} async-done(((bf16[4,64,768]{2,1,0:T(8,128)(2,1)}), bf16[4,64,768]{2,1,0:T(8,128)(2,1)S(1)}, u32[]{:S(2)}, u32[]{:S(2)}) %all-to-all-start.9) | async-done | bytes 393248 | tf_op jit(solution)/shard_map/all_to_all | solution.py:30
  238.2 11.7 %all_to_all.84 = bf16[4,64,768]{2,1,0:T(8,128)(2,1)S(1)} all-to-all(bf16[4,64,768]{2,1,0:T(8,128)(2,1)S(1)} %bitcast.439), channel_id=1, replica_groups=mesh['section'=2,'g'=8,'x'=4,'mp'=2] {'x'}, dimensions={0} | all-to-all | bytes 786432 | tf_op jit(solution)/shard_map/all_to_all | solution.py:30
  274.6 6.8 %all-to-all-done.8 = bf16[4,64,768]{2,1,0:T(8,128)(2,1)S(1)} async-done(((bf16[4,64,768]{2,1,0:T(8,128)(2,1)}), bf16[4,64,768]{2,1,0:T(8,128)(2,1)S(1)}, u32[]{:S(2)}, u32[]{:S(2)}) %all-to-all-start.8) | async-done | bytes 393248 | tf_op jit(solution)/shard_map/all_to_all | solution.py:30
  301.8 4.3 all-to-all-start.10
  307.2 7.6 %all-to-all-done.10 = bf16[4,64,768]{2,1,0:T(8,128)(2,1)} async-done(((bf16[4,64,768]{2,1,0:T(8,128)(2,1)}), bf16[4,64,768]{2,1,0:T(8,128)(2,1)}, u32[]{:S(2)}, u32[]{:S(2)}) %all-to-all-start.10) | async-done | bytes 393248 | tf_op jit(solution)/shard_map/all_to_all | solution.py:30
  322.5 3.9 concatenate.34
  329.3 3.9 fusion.15
  343.2 4.1 all-to-all-start.11
  347.4 4.3 pad_maximum_fusion.1
  351.6 4.4 all-to-all-done.11
  360.7 3.8 all-to-all-start.12
  385.8 5.9 %concatenate.35 = bf16[768,512]{0,1:T(8,128)(2,1)} concatenate(bf16[768,384]{0,1:T(8,128)(2,1)} %convolution_convert_fusion.8, bf16[768,1]{0,1:T(2,128)(2,1)S(1)} %stack.186, bf16[768,1]{0,1:T(2,128)(2,1)S(1)} %stack.187, bf16[768,4]{0,1:T(4,128)(2,1)S(1)} %convolution_convert_fusion.18, bf16[768,122]{0,1:T(8,128)(2,1)} %slice.218), dimensions={1} | concatenate | bytes 1572864 | tf_op jit(solution)/shard_map/concatenate | solution.py:240
  399.3 4.2 all-to-all-start.13
  405.8 8.9 %all-to-all-done.13 = bf16[4,8,24,512]{3,2,1,0:T(8,128)(2,1)} async-done(((bf16[4,8,24,512]{3,2,1,0:T(8,128)(2,1)}), bf16[4,8,24,512]{3,2,1,0:T(8,128)(2,1)}, u32[]{:S(2)}, u32[]{:S(2)}) %all-to-all-start.13) | async-done | bytes 786464 | tf_op jit(solution)/shard_map/all_to_all | solution.py:30
  420.4 4.4 all-to-all-start.14
  433.7 5.6 %collective-permute-done.27 = bf16[8,48]{0,1:T(8,128)(2,1)S(1)} collective-permute-done((bf16[8,48]{0,1:T(8,128)(2,1)S(1)}, bf16[8,48]{0,1:T(8,128)(2,1)S(1)}, u32[]{:S(2)}, u32[]{:S(2)}) %collective-permute-start.27) | collective-permute-done | bytes 800 | tf_op jit(solution)/shard_map/ppermute | solution.py:22
  439.4 9.5 %collective-permute-done.26 = bf16[8,48]{0,1:T(8,128)(2,1)S(1)} collective-permute-done((bf16[8,48]{0,1:T(8,128)(2,1)S(1)}, bf16[8,48]{0,1:T(8,128)(2,1)S(1)}, u32[]{:S(2)}, u32[]{:S(2)}) %collective-permute-start.26) | collective-permute-done | bytes 800 | tf_op jit(solution)/shard_map/ppermute | solution.py:22
  454.3 4.9 all-to-all-start.15
  461.8 19.1 %collective-permute-done.24 = bf16[197,768]{1,0:T(8,128)(2,1)S(1)} collective-permute-done((bf16[197,768]{1,0:T(8,128)(2,1)S(1)}, bf16[197,768]{1,0:T(8,128)(2,1)S(1)}, u32[]{:S(2)}, u32[]{:S(2)}) %collective-permute-start.24) | collective-permute-done | bytes 302624 | tf_op jit(solution)/shard_map/ppermute | solution.py:22
  497.6 8.9 %collective-permute-done.32 = bf16[4,2,24,1536]{3,2,0,1:T(8,128)(2,1)S(1)} collective-permute-done((bf16[4,2,24,1536]{3,2,0,1:T(8,128)(2,1)S(1)}, bf16[4,2,24,1536]{3,2,0,1:T(8,128)(2,1)S(1)}, u32[]{:S(2)}, u32[]{:S(2)}) %collective-permute-start.32) | collective-permute-done | bytes 589856 | tf_op jit(solution)/shard_map/ppermute | solution.py:22
  (487 shorter events, 202.6 us)
Async XLA Ops:
  7.2 156.4 %all-gather.2.cloned.1.call-start = ((), (), s32[]{:S(2)}) async-start(), calls=%async_computation.18 | async-start | bytes 10027008 | tf_op jit(solution)/shard_map/all_gather | solution.py:332
  69.8 33.0 %all-to-all-start.1 = ((bf16[4,8,24,1664]{3,2,1,0:T(8,128)(2,1)}), bf16[4,8,24,1664]{3,2,1,0:T(8,128)(2,1)S(1)}, u32[]{:S(2)}, u32[]{:S(2)}) async-start(bf16[4,8,24,1664]{3,2,1,0:T(8,128)(2,1)} %broadcast_in_dim.63), calls=%async_computation.1 | async-start | bytes 5111808 | tf_op jit(solution)/shard_map/all_to_all | solution.py:30
  126.2 34.6 %all-to-all-start.3 = ((bf16[4,8,24,1664]{3,2,1,0:T(8,128)(2,1)}), bf16[4,8,24,1664]{3,2,1,0:T(8,128)(2,1)S(1)}, u32[]{:S(2)}, u32[]{:S(2)}) async-start(bf16[4,8,24,1664]{3,2,1,0:T(8,128)(2,1)} %broadcast_in_dim.65), calls=%async_computation.3 | async-start | bytes 5111808 | tf_op jit(solution)/shard_map/all_to_all | solution.py:30
  129.8 32.6 %collective-permute-start.3 = (bf16[256,768]{1,0:T(8,128)(2,1)}, bf16[256,768]{1,0:T(8,128)(2,1)}, u32[]{:S(2)}, u32[]{:S(2)}) collective-permute-start(bf16[256,768]{1,0:T(8,128)(2,1)} %bitcast.434), channel_id=1, source_target_pairs={{0,1},{1,0},{2,3},{3,2},{4,5},{5,4},{6,7},{7,6},{8,9},{9,8},{10,11... | collective-permute-start | bytes 1179656 | tf_op jit(solution)/shard_map/ppermute | solution.py:22
  175.0 12.1 %all-to-all-start.5 = ((bf16[4,64,768]{2,1,0:T(8,128)(2,1)}), bf16[4,64,768]{2,1,0:T(8,128)(2,1)S(1)}, u32[]{:S(2)}, u32[]{:S(2)}) async-start(bf16[4,64,768]{2,1,0:T(8,128)(2,1)} %bitcast.40), calls=%async_computation.5 | async-start | bytes 786432 | tf_op jit(solution)/shard_map/all_to_all | solution.py:30
  222.3 12.1 %all-to-all-start.9 = ((bf16[4,64,768]{2,1,0:T(8,128)(2,1)}), bf16[4,64,768]{2,1,0:T(8,128)(2,1)S(1)}, u32[]{:S(2)}, u32[]{:S(2)}) async-start(bf16[4,64,768]{2,1,0:T(8,128)(2,1)} %bitcast.438), calls=%async_computation.9 | async-start | bytes 786432 | tf_op jit(solution)/shard_map/all_to_all | solution.py:30
  236.9 13.0 %collective-permute-start.11 = (f32[197,768]{1,0:T(8,128)S(1)}, f32[197,768]{1,0:T(8,128)S(1)}, u32[]{:S(2)}, u32[]{:S(2)}) collective-permute-start(f32[197,768]{1,0:T(8,128)S(1)} %convolution_bitcast_fusion), channel_id=1, source_target_pairs={{0,1},{1,0},{2,3},{3,2},{4,5},{5,4},{6,7},{7,6},{8,9},{9,8},{10,11... | collective-permute-start | bytes 1815560 | tf_op jit(solution)/shard_map/ppermute | solution.py:22
  250.9 21.7 %collective-permute-start.12 = (bf16[197,768]{1,0:T(8,128)(2,1)}, bf16[197,768]{1,0:T(8,128)(2,1)}, u32[]{:S(2)}, u32[]{:S(2)}) collective-permute-start(bf16[197,768]{1,0:T(8,128)(2,1)} %get-tuple-element.141), channel_id=1, source_target_pairs={{0,64},{64,0},{1,65},{65,1},{2,66},{66,2},{3,67},{67,3},{4,68},{68... | collective-permute-start | bytes 907784 | tf_op jit(solution)/shard_map/ppermute | solution.py:22
  269.2 12.2 %all-to-all-start.8 = ((bf16[4,64,768]{2,1,0:T(8,128)(2,1)}), bf16[4,64,768]{2,1,0:T(8,128)(2,1)S(1)}, u32[]{:S(2)}, u32[]{:S(2)}) async-start(bf16[4,64,768]{2,1,0:T(8,128)(2,1)} %bitcast.436), calls=%async_computation.8 | async-start | bytes 786432 | tf_op jit(solution)/shard_map/all_to_all | solution.py:30
  272.6 104.0 %reduce-scatter.3.cloned.1.call-start = ((), (), s32[]{:S(2)}) async-start(), calls=%async_computation.19 | async-start | bytes 5308416 | tf_op jit(solution)/shard_map/reduce_scatter | solution.py:210
  301.8 13.0 %all-to-all-start.10 = ((bf16[4,64,768]{2,1,0:T(8,128)(2,1)}), bf16[4,64,768]{2,1,0:T(8,128)(2,1)}, u32[]{:S(2)}, u32[]{:S(2)}) async-start(bf16[4,64,768]{2,1,0:T(8,128)(2,1)} %bitcast.452), calls=%async_computation.10 | async-start | bytes 786432 | tf_op jit(solution)/shard_map/all_to_all | solution.py:30
  314.8 13.4 %collective-permute-start.16 = (bf16[256,768]{1,0:T(8,128)(2,1)}, bf16[256,768]{1,0:T(8,128)(2,1)}, u32[]{:S(2)}, u32[]{:S(2)}) collective-permute-start(bf16[256,768]{1,0:T(8,128)(2,1)} %bitcast.78), channel_id=1, source_target_pairs={{0,1},{1,0},{2,3},{3,2},{4,5},{5,4},{6,7},{7,6},{8,9},{9,8},{10,11... | collective-permute-start | bytes 1179656 | tf_op jit(solution)/shard_map/ppermute | solution.py:22
  343.2 12.8 %all-to-all-start.11 = ((bf16[4,64,768]{2,1,0:T(8,128)(2,1)}), bf16[4,64,768]{2,1,0:T(8,128)(2,1)}, u32[]{:S(2)}, u32[]{:S(2)}) async-start(bf16[4,64,768]{2,1,0:T(8,128)(2,1)} %bitcast.437), calls=%async_computation.11 | async-start | bytes 786432 | tf_op jit(solution)/shard_map/all_to_all | solution.py:30
  347.3 134.9 %reduce-scatter.5.cloned.1.call-start = ((), (), s32[]{:S(2)}) async-start(), calls=%async_computation.20 | async-start | bytes 5308416 | tf_op jit(solution)/shard_map/reduce_scatter | solution.py:210
  358.3 6.2 %collective-permute-start.18 = (f32[197,768]{1,0:T(8,128)}, f32[197,768]{1,0:T(8,128)}, u32[]{:S(2)}, u32[]{:S(2)}) collective-permute-start(f32[197,768]{1,0:T(8,128)} %fusion.152), channel_id=1, source_target_pairs={{0,1},{1,0},{2,3},{3,2},{4,5},{5,4},{6,7},{7,6},{8,9},{9,8},{10,11... | collective-permute-start | bytes 1815560 | tf_op jit(solution)/shard_map/ppermute | solution.py:22
  360.7 36.5 %all-to-all-start.12 = ((bf16[4,8,24,1664]{3,2,1,0:T(8,128)(2,1)}), bf16[4,8,24,1664]{3,2,1,0:T(8,128)(2,1)S(1)}, u32[]{:S(2)}, u32[]{:S(2)}) async-start(bf16[4,8,24,1664]{3,2,1,0:T(8,128)(2,1)} %bitcast.388), calls=%async_computation.12 | async-start | bytes 5111808 | tf_op jit(solution)/shard_map/all_to_all | solution.py:30
  378.6 24.9 %collective-permute-start.22 = (bf16[2,24,1536]{2,1,0:T(8,128)(2,1)}, bf16[2,24,1536]{2,1,0:T(8,128)(2,1)}, u32[]{:S(2)}, u32[]{:S(2)}) collective-permute-start(bf16[2,24,1536]{2,1,0:T(8,128)(2,1)} %get-tuple-element.166), channel_id=1, source_target_pairs={{0,6},{2,4},{4,2},{6,0},{1,7},{3,5},{5,3},{7,1},{8,14},{10,12},{12... | collective-permute-start | bytes 442376 | tf_op jit(solution)/shard_map/ppermute | solution.py:22
  381.8 21.7 %collective-permute-start.21 = (bf16[2,24,1536]{2,1,0:T(8,128)(2,1)}, bf16[2,24,1536]{2,1,0:T(8,128)(2,1)}, u32[]{:S(2)}, u32[]{:S(2)}) collective-permute-start(bf16[2,24,1536]{2,1,0:T(8,128)(2,1)} %get-tuple-element.167), channel_id=1, source_target_pairs={{0,4},{2,6},{4,0},{6,2},{1,5},{3,7},{5,1},{7,3},{8,12},{10,14},{12... | collective-permute-start | bytes 442376 | tf_op jit(solution)/shard_map/ppermute | solution.py:22
  382.9 20.7 %collective-permute-start.20 = (bf16[2,24,1536]{2,1,0:T(8,128)(2,1)}, bf16[2,24,1536]{2,1,0:T(8,128)(2,1)}, u32[]{:S(2)}, u32[]{:S(2)}) collective-permute-start(bf16[2,24,1536]{2,1,0:T(8,128)(2,1)} %get-tuple-element.168), channel_id=1, source_target_pairs={{0,2},{2,0},{4,6},{6,4},{1,3},{3,1},{5,7},{7,5},{8,10},{10,8},{12,... | collective-permute-start | bytes 442376 | tf_op jit(solution)/shard_map/ppermute | solution.py:22
  399.3 15.4 %all-to-all-start.13 = ((bf16[4,8,24,512]{3,2,1,0:T(8,128)(2,1)}), bf16[4,8,24,512]{3,2,1,0:T(8,128)(2,1)}, u32[]{:S(2)}, u32[]{:S(2)}) async-start(bf16[4,8,24,512]{3,2,1,0:T(8,128)(2,1)} %copy.252), calls=%async_computation.13 | async-start | bytes 1572864 | tf_op jit(solution)/shard_map/all_to_all | solution.py:30
  418.1 9.4 %collective-permute-start.23 = (f32[197,768]{1,0:T(8,128)}, f32[197,768]{1,0:T(8,128)}, u32[]{:S(2)}, u32[]{:S(2)}) collective-permute-start(f32[197,768]{1,0:T(8,128)} %fusion.24), channel_id=1, source_target_pairs={{0,1},{1,0},{2,3},{3,2},{4,5},{5,4},{6,7},{7,6},{8,9},{9,8},{10,11... | collective-permute-start | bytes 1815560 | tf_op jit(solution)/shard_map/ppermute | solution.py:22
  420.4 28.8 %all-to-all-start.14 = ((bf16[4,8,24,1152]{3,2,1,0:T(8,128)(2,1)}), bf16[4,8,24,1152]{3,2,1,0:T(8,128)(2,1)}, u32[]{:S(2)}, u32[]{:S(2)}) async-start(bf16[4,8,24,1152]{3,2,1,0:T(8,128)(2,1)} %bitcast.405), calls=%async_computation.15 | async-start | bytes 3538944 | tf_op jit(solution)/shard_map/all_to_all | solution.py:30
  429.5 9.8 %collective-permute-start.27 = (bf16[8,48]{0,1:T(8,128)(2,1)S(1)}, bf16[8,48]{0,1:T(8,128)(2,1)S(1)}, u32[]{:S(2)}, u32[]{:S(2)}) collective-permute-start(bf16[8,48]{0,1:T(8,128)(2,1)S(1)} %get-tuple-element.172), channel_id=1, source_target_pairs={{0,6},{2,4},{4,2},{6,0},{1,7},{3,5},{5,3},{7,1},{8,14},{10,12},{12... | collective-permute-start | bytes 2312 | tf_op jit(solution)/shard_map/ppermute | solution.py:22
  432.8 16.1 %collective-permute-start.26 = (bf16[8,48]{0,1:T(8,128)(2,1)S(1)}, bf16[8,48]{0,1:T(8,128)(2,1)S(1)}, u32[]{:S(2)}, u32[]{:S(2)}) collective-permute-start(bf16[8,48]{0,1:T(8,128)(2,1)S(1)} %get-tuple-element.173), channel_id=1, source_target_pairs={{0,4},{2,6},{4,0},{6,2},{1,5},{3,7},{5,1},{7,3},{8,12},{10,14},{12... | collective-permute-start | bytes 2312 | tf_op jit(solution)/shard_map/ppermute | solution.py:22
  433.6 15.3 %collective-permute-start.25 = (bf16[8,48]{0,1:T(8,128)(2,1)S(1)}, bf16[8,48]{0,1:T(8,128)(2,1)S(1)}, u32[]{:S(2)}, u32[]{:S(2)}) collective-permute-start(bf16[8,48]{0,1:T(8,128)(2,1)S(1)} %get-tuple-element.171), channel_id=1, source_target_pairs={{0,2},{2,0},{4,6},{6,4},{1,3},{3,1},{5,7},{7,5},{8,10},{10,8},{12,... | collective-permute-start | bytes 2312 | tf_op jit(solution)/shard_map/ppermute | solution.py:22
  454.3 33.3 %all-to-all-start.15 = ((bf16[8,2,24,1664]{3,2,1,0:T(8,128)(2,1)}), bf16[8,2,24,1664]{3,2,1,0:T(8,128)(2,1)S(1)}, u32[]{:S(2)}, u32[]{:S(2)}) async-start(bf16[8,2,24,1664]{3,2,1,0:T(8,128)(2,1)} %pad_maximum_fusion.2), calls=%async_computation.16 | async-start | bytes 2555904 | tf_op jit(solution)/shard_map/all_to_all | solution.py:30
  459.6 21.3 %collective-permute-start.24 = (bf16[197,768]{1,0:T(8,128)(2,1)S(1)}, bf16[197,768]{1,0:T(8,128)(2,1)S(1)}, u32[]{:S(2)}, u32[]{:S(2)}) collective-permute-start(bf16[197,768]{1,0:T(8,128)(2,1)S(1)} %get-tuple-element.133), channel_id=1, source_target_pairs={{0,64},{64,0},{1,65},{65,1},{2,66},{66,2},{3,67},{67,3},{4,68},{68... | collective-permute-start | bytes 907784 | tf_op jit(solution)/shard_map/ppermute | solution.py:22
  483.4 8.7 %collective-permute-start.31 = (bf16[2,24,1536]{2,1,0:T(8,128)(2,1)S(1)}, bf16[2,24,1536]{2,1,0:T(8,128)(2,1)S(1)}, u32[]{:S(2)}, u32[]{:S(2)}) collective-permute-start(bf16[2,24,1536]{2,1,0:T(8,128)(2,1)S(1)} %get-tuple-element.162), channel_id=1, source_target_pairs={{0,6},{2,4},{4,2},{6,0},{1,7},{3,5},{5,3},{7,1},{8,14},{10,12},{12... | collective-permute-start | bytes 442376 | tf_op jit(solution)/shard_map/ppermute | solution.py:22
  484.7 7.5 %collective-permute-start.30 = (bf16[2,24,1536]{2,1,0:T(8,128)(2,1)S(1)}, bf16[2,24,1536]{2,1,0:T(8,128)(2,1)S(1)}, u32[]{:S(2)}, u32[]{:S(2)}) collective-permute-start(bf16[2,24,1536]{2,1,0:T(8,128)(2,1)S(1)} %get-tuple-element.163), channel_id=1, source_target_pairs={{0,4},{2,6},{4,0},{6,2},{1,5},{3,7},{5,1},{7,3},{8,12},{10,14},{12... | collective-permute-start | bytes 442376 | tf_op jit(solution)/shard_map/ppermute | solution.py:22
  486.1 6.6 %collective-permute-start.29 = (bf16[2,24,1536]{2,1,0:T(8,128)(2,1)S(1)}, bf16[2,24,1536]{2,1,0:T(8,128)(2,1)S(1)}, u32[]{:S(2)}, u32[]{:S(2)}) collective-permute-start(bf16[2,24,1536]{2,1,0:T(8,128)(2,1)S(1)} %get-tuple-element.164), channel_id=1, source_target_pairs={{0,2},{2,0},{4,6},{6,4},{1,3},{3,1},{5,7},{7,5},{8,10},{10,8},{12,... | collective-permute-start | bytes 442376 | tf_op jit(solution)/shard_map/ppermute | solution.py:22
  487.8 6.9 %collective-permute-start.28 = (f32[24,1664]{1,0:T(8,128)S(1)}, f32[24,1664]{1,0:T(8,128)S(1)}, u32[]{:S(2)}, u32[]{:S(2)}) collective-permute-start(f32[24,1664]{1,0:T(8,128)S(1)} %select_bitcast_fusion.4), channel_id=1, source_target_pairs={{0,64},{64,0},{1,65},{65,1},{2,66},{66,2},{3,67},{67,3},{4,68},{68... | collective-permute-start | bytes 479240 | tf_op jit(solution)/shard_map/ppermute | solution.py:22
  493.9 12.6 %collective-permute-start.32 = (bf16[4,2,24,1536]{3,2,0,1:T(8,128)(2,1)S(1)}, bf16[4,2,24,1536]{3,2,0,1:T(8,128)(2,1)S(1)}, u32[]{:S(2)}, u32[]{:S(2)}) collective-permute-start(bf16[4,2,24,1536]{3,2,0,1:T(8,128)(2,1)S(1)} %broadcast_select_fusion), channel_id=1, source_target_pairs={{0,64},{64,0},{1,65},{65,1},{2,66},{66,2},{3,67},{67,3},{4,68},{68... | collective-permute-start | bytes 1769480 | tf_op jit(solution)/shard_map/ppermute | solution.py:22
  (120 other events, 719.2 us)
Sparse Core Ops, SparseCore 0:
  23.9 122.3 all-gather.1
  282.3 81.8 reduce-scatter.2
  368.0 86.3 reduce-scatter.4
